TPU v7x, 128 devices: a whole 4x4x4 slice. The times are simulated.
128 devices in a mesh: dp: 4 (over z), feat: 32 (over y, x, core).
Axes of the slice: x: 4, y: 4, z: 4, core: 2. Of those that a mesh axis runs over, the one named last changes fastest.
Arguments:
- features: bfloat16 [1024, 16384], P('feat'), may hold values from -6 to 6
- targets: int32 [4, 4096], P('dp'), may hold values from 0 to 16383
- block_ids: int32 [4, 32, 16], P('dp'), may hold values from 0 to 127
- counts: int32 [4, 32], P('dp'), may hold values from 1 to 16, as said below
- target_slots: int32 [4, 4096], P('dp'), may hold values from 0 to 4095, each once within a row
- edge_tiles: bfloat16 [4, 32, 16, 128, 128], P('dp'), may hold values from -0.125 to 0.125
- self_weight: bfloat16 [1024, 256], P('feat'), may hold values from -0.1875 to 0.1875
- neigh_weight: bfloat16 [1024, 256], P('feat'), may hold values from -0.1875 to 0.1875
- hidden_bias: float32 [256], replicated, may hold values from -3 to 3
- hidden_grad: bfloat16 [4, 4096, 256], P('dp', 'feat'), may hold values from -6 to 6
Outputs:
- hidden: bfloat16 [4, 4096, 256], P('dp', 'feat')
- feature_grad: float32 [1024, 16384], P('feat')
- self_weight_grad: float32 [1024, 256], P('feat')
- neigh_weight_grad: float32 [1024, 256], P('feat')
- bias_grad: float32 [256], replicated
Inputs may be any that keep to these rules, and one draw needn't show every extreme that they name: `counts`: every group has a target block with 16 live slots and one with a single live slot.
All inputs are finite; a program needn't handle non-finite values.
Results may differ from a plain program's by a relative error of at most 0.0052.
Values may be sent and summed in bfloat16 or wider, within the bound.
No kernel may reach another device: no remote copies, remote signals or barrier semaphores. Data moves between devices by JAX's collectives and lax.ppermute only.
A program may use at most 128 MiB of HBM per device.

v0:
```python
import jax
import jax.numpy as jnp
from jax import lax
from jax.experimental import pallas as pl
from jax.experimental.pallas import tpu as pltpu
from jax.sharding import PartitionSpec as P

BLK = 128
MAXB = 16
TB = 32
NBLK = 128
TGT = 4096
NODES = 16384
COLS = 32
FEAT = 32
WIDE = 256
CHUNK = 4
PER = MAXB // CHUNK
UNROLL = 8
LIST = TB * PER + UNROLL
MIB = 1024 * 1024

F32 = jnp.float32
BF16 = jnp.bfloat16
NT = (((1,), (1,)), ((), ()))


def dot(left, right):
    return jnp.dot(left, right, preferred_element_type=F32)


def dot_nt(left, right):
    return lax.dot_general(left, right, NT, preferred_element_type=F32)


def one_hot_rows(low_row):
    n = low_row.shape[1]
    rows = lax.broadcasted_iota(jnp.int32, (WIDE, n), 0)
    return jnp.where(rows == low_row, 1.0, 0.0).astype(BF16)


def list_chunks(cnt_ref, tiles_ref, buf_ref, sem_ref, list_ref):
    def fetch(chunk):
        span = pl.ds(chunk * CHUNK, CHUNK)
        return pltpu.make_async_copy(tiles_ref.at[span], buf_ref.at[span], sem_ref.at[chunk])

    def block(b, total):
        chunks = (cnt_ref[b] + (CHUNK - 1)) // CHUNK
        for k in range(PER):
            list_ref[total + k] = b * PER + k

            @pl.when(k < chunks)
            def _():
                fetch(b * PER + k).start()

        return total + chunks

    total = lax.fori_loop(0, TB, block, jnp.int32(0))
    for u in range(UNROLL):
        list_ref[total + u] = 0

    def wait():
        def body(i, carry):
            fetch(list_ref[i]).wait()
            return carry

        lax.fori_loop(0, total, body, 0)

    return total, wait


def chunk_slots(bid_ref, cnt_ref, list_ref, item, total):
    chunk = list_ref[item]
    block = chunk // PER
    first = (chunk % PER) * CHUNK
    count = jnp.where(item < total, cnt_ref[block], 0)
    slots = [(bid_ref[chunk * CHUNK + j], first + j < count) for j in range(CHUNK)]
    return chunk, block, slots


def forward_kernel(
    bid_ref, cnt_ref, feat_ref, tgt_ref, slot_ref, tiles_ref,
    out_ref, tgtq_ref,
    buf_ref, sem_ref, list_ref, place_ref, agg_ref,
):
    total, wait = list_chunks(cnt_ref, tiles_ref, buf_ref, sem_ref, list_ref)

    slot = slot_ref[...]
    slot_hi = (slot // WIDE).astype(F32)
    slot_lo = slot % WIDE
    for i in range(TGT // WIDE):
        span = slice(i * WIDE, (i + 1) * WIDE)
        place_ref[:, span] = one_hot_rows(slot_lo[:, span])

    tgt = tgt_ref[...]
    row16 = lax.broadcasted_iota(jnp.int32, (16, TGT), 0)
    parts = jnp.where(row16 == 0, tgt // WIDE, jnp.where(row16 == 1, tgt % WIDE, 0)).astype(BF16)
    hi16 = jnp.broadcast_to(slot_hi, (16, TGT)).astype(BF16)

    def masked(values, wanted):
        reps = values.shape[0] // 16
        mask = hi16 == jnp.asarray(wanted, BF16)
        pieces = [
            jnp.where(mask, values[r * 16:(r + 1) * 16], jnp.zeros((), BF16)) for r in range(reps)
        ]
        return pieces

    rows = []
    for q in range(TGT // WIDE):
        rows += masked(parts, q)
    moved = dot_nt(jnp.concatenate(rows, axis=0), place_ref[...])
    for q in range(TGT // WIDE):
        tgtq_ref[:, q * WIDE:(q + 1) * WIDE] = moved[q * 16:q * 16 + 8]

    group = 32

    def gather(i, carry):
        span = pl.ds(pl.multiple_of(i * WIDE, WIDE), WIDE)
        ids = tgtq_ref[:, span]
        high = jnp.broadcast_to(ids[0:1], (8, WIDE))
        marks = one_hot_rows(ids[1:2].astype(jnp.int32))
        acc = [jnp.zeros((8, WIDE), F32) for _ in range(COLS // 8)]
        for g in range(NODES // WIDE // group):
            left = jnp.concatenate(
                [
                    feat_ref[:, (g * group + n) * WIDE:(g * group + n + 1) * WIDE]
                    for n in range(group)
                ],
                axis=0,
            )
            prod = dot(left, marks)
            for n in range(group):
                mask = high == float(g * group + n)
                for c in range(COLS // 8):
                    at = n * COLS + c * 8
                    acc[c] = jnp.where(mask, prod[at:at + 8], acc[c])
        own = jnp.concatenate(acc, axis=0).astype(BF16)
        out_ref[2 * i, 0:COLS] = own[:, :BLK]
        out_ref[2 * i + 1, 0:COLS] = own[:, BLK:]
        return carry

    lax.fori_loop(0, TGT // WIDE, gather, 0)

    agg_ref[...] = jnp.zeros_like(agg_ref)
    wait()

    def aggregate(i, carry):
        done = []
        for u in range(UNROLL):
            chunk, block, slots = chunk_slots(bid_ref, cnt_ref, list_ref, i * UNROLL + u, total)
            left = []
            for node_block, live in slots:
                span = pl.ds(pl.multiple_of(node_block * BLK, BLK), BLK)
                left.append(jnp.where(live, feat_ref[:, span], jnp.zeros((), BF16)))
            tiles = buf_ref[pl.ds(chunk * CHUNK, CHUNK)].reshape(CHUNK * BLK, BLK)
            done.append((block, dot(jnp.concatenate(left, axis=1), tiles)))
        for block, prod in done:
            span = pl.ds(pl.multiple_of(block * BLK, BLK), BLK)
            agg_ref[:, span] += prod
        return carry

    lax.fori_loop(0, (total + UNROLL - 1) // UNROLL, aggregate, 0)

    aggregate_rows = agg_ref[...].astype(BF16)
    half = 8
    for g in range(TGT // WIDE // half):
        rows = []
        for q in range(half):
            rows += masked(aggregate_rows, g * half + q)
        moved = dot_nt(jnp.concatenate(rows, axis=0), place_ref[...]).astype(BF16)
        for q in range(half):
            piece = moved[q * COLS:(q + 1) * COLS]
            out_ref[2 * (g * half + q), COLS:] = piece[:, :BLK]
            out_ref[2 * (g * half + q) + 1, COLS:] = piece[:, BLK:]


VMEM = pl.BlockSpec(memory_space=pltpu.VMEM)
SMEM = pl.BlockSpec(memory_space=pltpu.SMEM)
HBM = pl.BlockSpec(memory_space=pl.ANY)


def params(mib):
    return pltpu.CompilerParams(vmem_limit_bytes=mib * MIB)


def forward(block_list, counts, features, targets, slots, tiles):
    return pl.pallas_call(
        forward_kernel,
        out_shape=(
            jax.ShapeDtypeStruct((FEAT, 2 * COLS, BLK), BF16),
            jax.ShapeDtypeStruct((8, TGT), F32),
        ),
        in_specs=[SMEM, SMEM, VMEM, VMEM, VMEM, HBM],
        out_specs=(VMEM, VMEM),
        scratch_shapes=[
            pltpu.VMEM((TB * MAXB, BLK, BLK), BF16),
            pltpu.SemaphoreType.DMA((TB * PER,)),
            pltpu.SMEM((LIST,), jnp.int32),
            pltpu.VMEM((WIDE, TGT), BF16),
            pltpu.VMEM((COLS, TGT), F32),
        ],
        compiler_params=params(48),
        name="gather_and_aggregate",
    )(block_list, counts, features, targets, slots, tiles)


def middle_kernel(x_ref, w_ref, bias_ref, grad_ref, hidden_ref, back_ref, wgrad_ref):
    x = x_ref[...].reshape(FEAT * 2 * COLS, BLK)
    w = w_ref[...]
    preact = lax.dot_general(x, w, (((0,), (0,)), ((), ())), preferred_element_type=F32)
    preact = preact + bias_ref[...]
    sig = jax.nn.sigmoid(preact)
    hidden_ref[...] = (preact * sig).astype(BF16)
    slope = (grad_ref[...].astype(F32) * sig * (1.0 + preact * (1.0 - sig))).astype(BF16)
    back_ref[...] = dot_nt(w, slope).astype(BF16).reshape(FEAT, 2 * COLS, BLK)
    wgrad_ref[:, :2 * COLS, :] = dot(x, slope).astype(BF16).reshape(FEAT, 2 * COLS, WIDE)
    total = jnp.sum(slope.astype(F32), axis=0, keepdims=True)
    first = total.astype(BF16)
    rest = total - first.astype(F32)
    second = rest.astype(BF16)
    third = (rest - second.astype(F32)).astype(BF16)
    row = lax.broadcasted_iota(jnp.int32, (16, WIDE), 0)
    tail = jnp.where(
        row == 0,
        first.astype(F32),
        jnp.where(row == 1, second.astype(F32), jnp.where(row == 2, third.astype(F32), 0.0)),
    ).astype(BF16)
    wgrad_ref[:, 2 * COLS:, :] = jnp.broadcast_to(tail[None], (FEAT, 16, WIDE))


def middle(x, w, bias, grad):
    return pl.pallas_call(
        middle_kernel,
        out_shape=(
            jax.ShapeDtypeStruct((BLK, WIDE), BF16),
            jax.ShapeDtypeStruct((FEAT, 2 * COLS, BLK), BF16),
            jax.ShapeDtypeStruct((FEAT, 2 * COLS + 16, WIDE), BF16),
        ),
        in_specs=[VMEM] * 4,
        out_specs=(VMEM,) * 3,
        compiler_params=params(32),
        name="hidden_and_slope",
    )(x, w, bias, grad)


def backward_kernel(
    zid_ref, bid_ref, cnt_ref, back_ref, slot_ref, tgtq_ref, tiles_ref,
    near_ref, far_ref,
    buf_ref, sem_ref, list_ref, rows_ref, grad_ref, mark_ref,
):
    total, wait = list_chunks(cnt_ref, tiles_ref, buf_ref, sem_ref, list_ref)

    slot = slot_ref[...]
    slot_hi = (slot // WIDE).astype(F32)
    slot_lo = slot % WIDE
    pairs = TGT // WIDE

    left = jnp.concatenate(
        [
            jnp.concatenate([back_ref[2 * q, COLS:], back_ref[2 * q + 1, COLS:]], axis=1)
            for q in range(pairs)
        ],
        axis=0,
    )
    for i in range(TGT // WIDE):
        span = slice(i * WIDE, (i + 1) * WIDE)
        prod = dot(left, one_hot_rows(slot_lo[:, span]))
        high = jnp.broadcast_to(slot_hi[:, span], (8, WIDE))
        acc = [jnp.zeros((8, WIDE), F32) for _ in range(COLS // 8)]
        for q in range(pairs):
            mask = high == float(q)
            for c in range(COLS // 8):
                at = q * COLS + c * 8
                acc[c] = jnp.where(mask, prod[at:at + 8], acc[c])
        rows_ref[:, span] = jnp.concatenate(acc, axis=0).astype(BF16)

    grad_ref[...] = jnp.zeros_like(grad_ref)
    wait()

    def spread(i, carry):
        done = []
        for u in range(UNROLL):
            chunk, block, slots = chunk_slots(bid_ref, cnt_ref, list_ref, i * UNROLL + u, total)
            span = pl.ds(pl.multiple_of(block * BLK, BLK), BLK)
            tiles = buf_ref[pl.ds(chunk * CHUNK, CHUNK)].reshape(CHUNK * BLK, BLK)
            done.append((slots, dot_nt(rows_ref[:, span], tiles)))
        for slots, prod in done:
            for j, (node_block, live) in enumerate(slots):
                piece = prod[:, j * BLK:(j + 1) * BLK]
                span = pl.ds(pl.multiple_of(node_block * BLK, BLK), BLK)
                grad_ref[:, span] += jnp.where(live, piece, 0.0)
        return carry

    lax.fori_loop(0, (total + UNROLL - 1) // UNROLL, spread, 0)

    ids = tgtq_ref[...]
    for i in range(TGT // WIDE):
        span = slice(i * WIDE, (i + 1) * WIDE)
        mark_ref[:, span] = one_hot_rows(ids[1:2, span].astype(jnp.int32))
    hi16 = jnp.broadcast_to(ids[0:1], (16, TGT)).astype(BF16)
    own = jnp.concatenate([back_ref[q, :COLS] for q in range(FEAT)], axis=1)
    quarter = NODES // 4
    per = quarter // WIDE
    half = 8

    def scatter(step, carry):
        which = lax.rem(zid_ref[0] + step, 4)
        for g in range(per // half):
            rows = []
            for n in range(half):
                wanted = (which * per + g * half + n).astype(F32).astype(BF16)
                mask = hi16 == wanted
                for r in range(COLS // 16):
                    rows.append(
                        jnp.where(mask, own[r * 16:(r + 1) * 16], jnp.zeros((), BF16))
                    )
            prod = dot_nt(jnp.concatenate(rows, axis=0), mark_ref[...])
            for n in range(half):
                at = (g * half + n) * WIDE
                span = pl.ds(pl.multiple_of(which * quarter + at, WIDE), WIDE)
                value = grad_ref[:, span] + prod[n * COLS:(n + 1) * COLS]

                @pl.when(step == 0)
                def _():
                    near_ref[:, at:at + WIDE] = value

                @pl.when(step > 0)
                def _():
                    far_ref[jnp.maximum(step - 1, 0), :, at:at + WIDE] = value.astype(BF16)

        return carry

    lax.fori_loop(0, 4, scatter, 0)


def backward(zid, block_list, counts, back, slots, tgtq, tiles):
    return pl.pallas_call(
        backward_kernel,
        out_shape=(
            jax.ShapeDtypeStruct((COLS, NODES // 4), F32),
            jax.ShapeDtypeStruct((3, COLS, NODES // 4), BF16),
        ),
        in_specs=[SMEM, SMEM, SMEM, VMEM, VMEM, VMEM, HBM],
        out_specs=(VMEM, VMEM),
        scratch_shapes=[
            pltpu.VMEM((TB * MAXB, BLK, BLK), BF16),
            pltpu.SemaphoreType.DMA((TB * PER,)),
            pltpu.SMEM((LIST,), jnp.int32),
            pltpu.VMEM((COLS, TGT), BF16),
            pltpu.VMEM((COLS, NODES), F32),
            pltpu.VMEM((WIDE, TGT), BF16),
        ],
        compiler_params=params(48),
        name="spread_and_scatter",
    )(zid, block_list, counts, back, slots, tgtq, tiles)


def place_kernel(zid_ref, a_ref, b_ref, c_ref, d_ref, out_ref):
    quarter = NODES // 4
    for step, ref in enumerate((a_ref, b_ref, c_ref, d_ref)):
        at = pl.multiple_of(lax.rem(zid_ref[0] + step, 4) * quarter, quarter)
        out_ref[:, pl.ds(at, quarter)] = ref[...].astype(F32)


def place(zid, quarters):
    return pl.pallas_call(
        place_kernel,
        out_shape=jax.ShapeDtypeStruct((COLS, NODES), F32),
        in_specs=[SMEM] + [VMEM] * 4,
        out_specs=VMEM,
        compiler_params=params(32),
        name="place_quarters",
    )(zid, *quarters)


def shift(value, by):
    return lax.ppermute(value, "dp", [(k, (k + by) % 4) for k in range(4)])


def shards(
    features,
    targets,
    block_ids,
    counts,
    target_slots,
    edge_tiles,
    self_weight,
    neigh_weight,
    hidden_bias,
    hidden_grad,
):
    tiles = edge_tiles.reshape(TB * MAXB, BLK, BLK)
    block_list = block_ids.reshape(-1)
    live = counts.reshape(-1)
    zid = lax.axis_index("dp").astype(jnp.int32).reshape(1)

    weights = lax.all_gather(
        jnp.concatenate([self_weight, neigh_weight], axis=0), "feat", axis=0, tiled=True
    )
    sent, tgtq = forward(block_list, live, features, targets, target_slots, tiles)
    got = lax.all_to_all(sent, "feat", 0, 0, tiled=True)
    hidden, back, wgrad = middle(got, weights, hidden_bias.reshape(1, -1), hidden_grad[0])
    back = lax.all_to_all(back, "feat", 0, 0, tiled=True)
    near, far = backward(zid, block_list, live, back, target_slots, tgtq, tiles)

    wgrad = lax.all_to_all(wgrad, "feat", 0, 0, tiled=True)
    wsum = jnp.sum(wgrad.astype(F32), axis=0)
    wsum = (wsum + shift(wsum, 2)) + (shift(wsum, 1) + shift(wsum, 3))
    self_grad = wsum[:COLS]
    neigh_grad = wsum[COLS:2 * COLS]
    bias_grad = wsum[2 * COLS] + (wsum[2 * COLS + 1] + wsum[2 * COLS + 2])

    one, two, three = shift(far[0], 1), shift(far[1], 2), shift(far[2], 3)
    done = (near + one.astype(F32) + two.astype(F32) + three.astype(F32)).astype(BF16)
    feature_grad = place(zid, (done, shift(done, 3), shift(done, 2), shift(done, 1)))
    return (hidden[None], feature_grad, self_grad, neigh_grad, bias_grad)


def solution(mesh):
    return jax.shard_map(
        shards,
        mesh=mesh,
        in_specs=(
            P("feat", None),
            P("dp", None),
            P("dp", None, None),
            P("dp", None),
            P("dp", None),
            P("dp", None, None, None, None),
            P("feat", None),
            P("feat", None),
            P(),
            P("dp", "feat", None),
        ),
        out_specs=(P("dp", "feat", None), P("feat", None), P("feat", None), P("feat", None), P()),
        check_vma=False,
    )
```

profile of v0, /device:TPU:0, one launch (start us, length us, event | category | flops | bytes accessed | tf_op | source)
XLA Modules:
  0.0 144.2 jit_solution(5141374941486651355)
XLA Ops:
  7.2 1.4 pad_maximum_fusion
  8.6 0.8 copy.15
  9.4 1.2 copy-done
  10.7 0.7 copy-done.3
  11.4 0.7 copy-done.5
  12.1 0.7 copy-done.6
  12.8 16.0 %gather_and_aggregate.1 = (bf16[32,64,128]{2,1,0:T(8,128)(2,1)S(1)}, f32[8,4096]{1,0:T(8,128)S(1)}) custom-call(s32[512]{0:T(512)S(1)} %reshape.27.bid_ref, s32[32]{0:T(128)S(1)} %bitcast.14, bf16[32,16384]{1,0:T(8,128)(2,1)S(1)} %copy-done, s32[1,4096]{1,0:T(1,128)S(1)} %copy-done.5, s32[1,4096]{1,0:T(1,128)S(1)} %copy-done.3, bf16[512,128,128]{2,1,0:T(8,128)(2,1)} %bitcast.17), custom_call_target="tpu_custom_call" | custom-call | tf_op jit(solution)/shard_map/gather_and_aggregate/pallas_call | solution.py:187
  28.8 19.0 %all_to_all.15.x_ref = bf16[32,64,128]{2,1,0:T(8,128)(2,1)S(1)} all-to-all(bf16[32,64,128]{2,1,0:T(8,128)(2,1)S(1)} %get-tuple-element.12), channel_id=1, replica_groups=mesh['dp'=4,'feat'=32] {'feat'}, dimensions={0} | all-to-all | bytes 1048576 | tf_op jit(solution)/shard_map/all_to_all | solution.py:401
  47.7 8.5 %all-gather.2.cloned.1.call-done.w_ref = bf16[2048,256]{1,0:T(8,128)(2,1)} async-done(((bf16[64,256]{1,0:T(8,128)(2,1)}), bf16[2048,256]{1,0:T(8,128)(2,1)}) %all-gather.2.cloned.1.call-update) | async-done | bytes 1048592 | tf_op jit(solution)/shard_map/all_gather | solution.py:397
  56.3 1.2 copy-done.1
  57.5 2.4 %hidden_and_slope.1 = (bf16[128,256]{1,0:T(8,128)(2,1)}, bf16[32,64,128]{2,1,0:T(8,128)(2,1)}, bf16[32,80,256]{2,1,0:T(8,128)(2,1)}) custom-call(bf16[32,64,128]{2,1,0:T(8,128)(2,1)S(1)} %all_to_all.15.x_ref, bf16[2048,256]{1,0:T(8,128)(2,1)S(1)} %copy-done.1, f32[1,256]{1,0:T(1,128)S(1)} %bitcast.16, bf16[128,256]{1,0:T(8,128)(2,1)S(1)} %bitcast.13), custom_call_target="tpu_custom_call" | custom-call | tf_op jit(solution)/shard_map/hidden_and_slope/pallas_call | solution.py:232
  59.8 4.9 %all-to-all-start.1 = ((bf16[32,64,128]{2,1,0:T(8,128)(2,1)}), bf16[32,64,128]{2,1,0:T(8,128)(2,1)S(1)}, u32[]{:S(2)}, u32[]{:S(2)}) async-start(bf16[32,64,128]{2,1,0:T(8,128)(2,1)} %get-tuple-element.14), calls=%async_computation.1 | async-start | bytes 1048576 | tf_op jit(solution)/shard_map/all_to_all | solution.py:403
  64.8 11.8 %all-to-all-done.1.back_ref = bf16[32,64,128]{2,1,0:T(8,128)(2,1)S(1)} async-done(((bf16[32,64,128]{2,1,0:T(8,128)(2,1)}), bf16[32,64,128]{2,1,0:T(8,128)(2,1)S(1)}, u32[]{:S(2)}, u32[]{:S(2)}) %all-to-all-start.1) | async-done | bytes 524320 | tf_op jit(solution)/shard_map/all_to_all | solution.py:403
  76.5 20.9 %spread_and_scatter.1 = (f32[32,4096]{1,0:T(8,128)S(1)}, bf16[3,32,4096]{2,1,0:T(8,128)(2,1)S(1)}) custom-call(s32[1]{0:T(128)} %bitcast.5.zid_ref, s32[512]{0:T(512)S(1)} %reshape.27.bid_ref, s32[32]{0:T(128)S(1)} %bitcast.15, bf16[32,64,128]{2,1,0:T(8,128)(2,1)S(1)} %all-to-all-done.1.back_ref, s32[1,4096]{1,0:T(1,128)S(1)} %copy-done.4, ...), custom_call_target="tpu_custom_call" | custom-call | tf_op jit(solution)/shard_map/spread_and_scatter/pallas_call | solution.py:337
  97.5 1.5 %collective-permute-start = (bf16[32,4096]{1,0:T(8,128)(2,1)S(1)}, bf16[32,4096]{1,0:T(8,128)(2,1)S(1)}, u32[]{:S(2)}, u32[]{:S(2)}) collective-permute-start(bf16[32,4096]{1,0:T(8,128)(2,1)S(1)} %get-tuple-element.19), channel_id=1, source_target_pairs={{0,32},{32,64},{64,96},{96,0},{1,33},{33,65},{65,97},{97,1},{2,34}... | collective-permute-start | bytes 786440 | tf_op jit(solution)/shard_map/ppermute | solution.py:377
  99.0 1.8 %collective-permute-start.2 = (bf16[32,4096]{1,0:T(8,128)(2,1)S(1)}, bf16[32,4096]{1,0:T(8,128)(2,1)S(1)}, u32[]{:S(2)}, u32[]{:S(2)}) collective-permute-start(bf16[32,4096]{1,0:T(8,128)(2,1)S(1)} %get-tuple-element.20), channel_id=1, source_target_pairs={{0,96},{32,0},{64,32},{96,64},{1,97},{33,1},{65,33},{97,65},{2,98}... | collective-permute-start | bytes 786440 | tf_op jit(solution)/shard_map/ppermute | solution.py:377
  100.8 2.3 %collective-permute-start.1 = (bf16[32,4096]{1,0:T(8,128)(2,1)S(1)}, bf16[32,4096]{1,0:T(8,128)(2,1)S(1)}, u32[]{:S(2)}, u32[]{:S(2)}) collective-permute-start(bf16[32,4096]{1,0:T(8,128)(2,1)S(1)} %get-tuple-element.21), channel_id=1, source_target_pairs={{0,64},{32,96},{64,0},{96,32},{1,65},{33,97},{65,1},{97,33},{2,66}... | collective-permute-start | bytes 786440 | tf_op jit(solution)/shard_map/ppermute | solution.py:377
  103.2 4.0 %all-to-all-start.2 = ((bf16[32,80,256]{2,1,0:T(8,128)(2,1)}), bf16[32,80,256]{2,1,0:T(8,128)(2,1)S(1)}, u32[]{:S(2)}, u32[]{:S(2)}) async-start(bf16[32,80,256]{2,1,0:T(8,128)(2,1)} %get-tuple-element.18), calls=%async_computation.2 | async-start | bytes 2621440 | tf_op jit(solution)/shard_map/all_to_all | solution.py:406
  107.2 1.0 collective-permute-done.2
  108.2 5.2 %collective-permute-done.1 = bf16[32,4096]{1,0:T(8,128)(2,1)S(1)} collective-permute-done((bf16[32,4096]{1,0:T(8,128)(2,1)S(1)}, bf16[32,4096]{1,0:T(8,128)(2,1)S(1)}, u32[]{:S(2)}, u32[]{:S(2)}) %collective-permute-start.1) | collective-permute-done | bytes 262176 | tf_op jit(solution)/shard_map/ppermute | solution.py:377
  113.5 1.4 collective-permute-start.5
  114.9 2.4 %collective-permute-start.4 = (bf16[32,4096]{1,0:T(8,128)(2,1)S(1)}, bf16[32,4096]{1,0:T(8,128)(2,1)S(1)}, u32[]{:S(2)}, u32[]{:S(2)}) collective-permute-start(bf16[32,4096]{1,0:T(8,128)(2,1)S(1)} %add_convert_fusion.a_ref), channel_id=1, source_target_pairs={{0,64},{32,96},{64,0},{96,32},{1,65},{33,97},{65,1},{97,33},{2,66}... | collective-permute-start | bytes 786440 | tf_op jit(solution)/shard_map/ppermute | solution.py:377
  117.3 0.6 collective-permute-start.3
  117.9 10.1 %all-to-all-done.2 = bf16[32,80,256]{2,1,0:T(8,128)(2,1)S(1)} async-done(((bf16[32,80,256]{2,1,0:T(8,128)(2,1)}), bf16[32,80,256]{2,1,0:T(8,128)(2,1)S(1)}, u32[]{:S(2)}, u32[]{:S(2)}) %all-to-all-start.2) | async-done | bytes 1310752 | tf_op jit(solution)/shard_map/all_to_all | solution.py:406
  128.1 0.7 collective-permute-start.8
  128.8 1.4 collective-permute-start.7
  130.2 1.2 collective-permute-start.6
  131.4 1.5 %place_quarters.1 = f32[32,16384]{1,0:T(8,128)} custom-call(s32[1]{0:T(128)} %bitcast.5.zid_ref, bf16[32,4096]{1,0:T(8,128)(2,1)S(1)} %add_convert_fusion.a_ref, bf16[32,4096]{1,0:T(8,128)(2,1)S(1)} %collective-permute-done.3.b_ref, bf16[32,4096]{1,0:T(8,128)(2,1)S(1)} %collective-permute-done.4.c_ref, bf16[32,4096]{1,0:T(8,128)(2,1)S(1)} %collective-permute-done.5.d_ref), custom_call_target="tpu_custom_call" | custom-call | tf_op jit(solution)/shard_map/place_quarters/pallas_call | solution.py:366
  133.2 1.3 collective-permute-done.7
  134.4 1.7 %collective-permute-done.6 = f32[80,256]{1,0:T(8,128)S(1)} collective-permute-done((f32[80,256]{1,0:T(8,128)S(1)}, f32[80,256]{1,0:T(8,128)S(1)}, u32[]{:S(2)}, u32[]{:S(2)}) %collective-permute-start.6) | collective-permute-done | bytes 81952 | tf_op jit(solution)/shard_map/ppermute | solution.py:377
  136.2 0.6 fusion
  136.7 0.6 fusion.1
  (25 shorter events, 1.0 us)
Async XLA Ops:
  7.2 49.1 %all-gather.2.cloned.1.call-start = ((), (), s32[]{:S(2)}) async-start(), calls=%async_computation.3 | async-start | bytes 1081344 | tf_op jit(solution)/shard_map/all_gather | solution.py:397
  9.4 1.2 copy-start
  10.7 0.7 copy-start.3
  11.4 0.7 copy-start.5
  12.1 0.7 copy-start.6
  12.8 43.5 %copy-start.2 = (bf16[1,128,256]{2,1,0:T(8,128)(2,1)S(1)}, bf16[1,128,256]{2,1,0:T(8,128)(2,1)}, u32[]{:S(2)}) copy-start(bf16[1,128,256]{2,1,0:T(8,128)(2,1)} %param.19) | copy-start | bytes 196612
  12.8 43.5 %copy-start.8 = (f32[256]{0:T(256)S(1)}, f32[256]{0:T(256)}, u32[]{:S(2)}) copy-start(f32[256]{0:T(256)} %param.18) | copy-start | bytes 3076
  28.8 47.8 %copy-start.4 = (s32[1,4096]{1,0:T(1,128)S(1)}, s32[1,4096]{1,0:T(1,128)}, u32[]{:S(2)}) copy-start(s32[1,4096]{1,0:T(1,128)} %slot_ref.3) | copy-start | bytes 49156
  28.8 47.8 %copy-start.7 = (s32[1,32]{1,0:T(1,128)S(1)}, s32[1,32]{1,0:T(1,128)}, u32[]{:S(2)}) copy-start(s32[1,32]{1,0:T(1,128)} %param.13) | copy-start | bytes 388
  56.2 1.2 copy-start.1
  59.8 16.7 %all-to-all-start.1 = ((bf16[32,64,128]{2,1,0:T(8,128)(2,1)}), bf16[32,64,128]{2,1,0:T(8,128)(2,1)S(1)}, u32[]{:S(2)}, u32[]{:S(2)}) async-start(bf16[32,64,128]{2,1,0:T(8,128)(2,1)} %get-tuple-element.14), calls=%async_computation.1 | async-start | bytes 1048576 | tf_op jit(solution)/shard_map/all_to_all | solution.py:403
  97.5 9.7 %collective-permute-start = (bf16[32,4096]{1,0:T(8,128)(2,1)S(1)}, bf16[32,4096]{1,0:T(8,128)(2,1)S(1)}, u32[]{:S(2)}, u32[]{:S(2)}) collective-permute-start(bf16[32,4096]{1,0:T(8,128)(2,1)S(1)} %get-tuple-element.19), channel_id=1, source_target_pairs={{0,32},{32,64},{64,96},{96,0},{1,33},{33,65},{65,97},{97,1},{2,34}... | collective-permute-start | bytes 786440 | tf_op jit(solution)/shard_map/ppermute | solution.py:377
  99.0 9.2 %collective-permute-start.2 = (bf16[32,4096]{1,0:T(8,128)(2,1)S(1)}, bf16[32,4096]{1,0:T(8,128)(2,1)S(1)}, u32[]{:S(2)}, u32[]{:S(2)}) collective-permute-start(bf16[32,4096]{1,0:T(8,128)(2,1)S(1)} %get-tuple-element.20), channel_id=1, source_target_pairs={{0,96},{32,0},{64,32},{96,64},{1,97},{33,1},{65,33},{97,65},{2,98}... | collective-permute-start | bytes 786440 | tf_op jit(solution)/shard_map/ppermute | solution.py:377
  100.8 12.6 %collective-permute-start.1 = (bf16[32,4096]{1,0:T(8,128)(2,1)S(1)}, bf16[32,4096]{1,0:T(8,128)(2,1)S(1)}, u32[]{:S(2)}, u32[]{:S(2)}) collective-permute-start(bf16[32,4096]{1,0:T(8,128)(2,1)S(1)} %get-tuple-element.21), channel_id=1, source_target_pairs={{0,64},{32,96},{64,0},{96,32},{1,65},{33,97},{65,1},{97,33},{2,66}... | collective-permute-start | bytes 786440 | tf_op jit(solution)/shard_map/ppermute | solution.py:377
  103.2 24.8 %all-to-all-start.2 = ((bf16[32,80,256]{2,1,0:T(8,128)(2,1)}), bf16[32,80,256]{2,1,0:T(8,128)(2,1)S(1)}, u32[]{:S(2)}, u32[]{:S(2)}) async-start(bf16[32,80,256]{2,1,0:T(8,128)(2,1)} %get-tuple-element.18), calls=%async_computation.2 | async-start | bytes 2621440 | tf_op jit(solution)/shard_map/all_to_all | solution.py:406
  113.5 16.7 %collective-permute-start.5 = (bf16[32,4096]{1,0:T(8,128)(2,1)S(1)}, bf16[32,4096]{1,0:T(8,128)(2,1)S(1)}, u32[]{:S(2)}, u32[]{:S(2)}) collective-permute-start(bf16[32,4096]{1,0:T(8,128)(2,1)S(1)} %add_convert_fusion.a_ref), channel_id=1, source_target_pairs={{0,32},{32,64},{64,96},{96,0},{1,33},{33,65},{65,97},{97,1},{2,34}... | collective-permute-start | bytes 786440 | tf_op jit(solution)/shard_map/ppermute | solution.py:377
  114.9 16.5 %collective-permute-start.4 = (bf16[32,4096]{1,0:T(8,128)(2,1)S(1)}, bf16[32,4096]{1,0:T(8,128)(2,1)S(1)}, u32[]{:S(2)}, u32[]{:S(2)}) collective-permute-start(bf16[32,4096]{1,0:T(8,128)(2,1)S(1)} %add_convert_fusion.a_ref), channel_id=1, source_target_pairs={{0,64},{32,96},{64,0},{96,32},{1,65},{33,97},{65,1},{97,33},{2,66}... | collective-permute-start | bytes 786440 | tf_op jit(solution)/shard_map/ppermute | solution.py:377
  117.3 14.1 %collective-permute-start.3 = (bf16[32,4096]{1,0:T(8,128)(2,1)S(1)}, bf16[32,4096]{1,0:T(8,128)(2,1)S(1)}, u32[]{:S(2)}, u32[]{:S(2)}) collective-permute-start(bf16[32,4096]{1,0:T(8,128)(2,1)S(1)} %add_convert_fusion.a_ref), channel_id=1, source_target_pairs={{0,96},{32,0},{64,32},{96,64},{1,97},{33,1},{65,33},{97,65},{2,98}... | collective-permute-start | bytes 786440 | tf_op jit(solution)/shard_map/ppermute | solution.py:377
  128.1 5.1 %collective-permute-start.8 = (f32[80,256]{1,0:T(8,128)S(1)}, f32[80,256]{1,0:T(8,128)S(1)}, u32[]{:S(2)}, u32[]{:S(2)}) collective-permute-start(f32[80,256]{1,0:T(8,128)S(1)} %convert_reduce_fusion), channel_id=1, source_target_pairs={{0,96},{32,0},{64,32},{96,64},{1,97},{33,1},{65,33},{97,65},{2,98}... | collective-permute-start | bytes 245768 | tf_op jit(solution)/shard_map/ppermute | solution.py:377
  128.8 5.7 %collective-permute-start.7 = (f32[80,256]{1,0:T(8,128)S(1)}, f32[80,256]{1,0:T(8,128)S(1)}, u32[]{:S(2)}, u32[]{:S(2)}) collective-permute-start(f32[80,256]{1,0:T(8,128)S(1)} %convert_reduce_fusion), channel_id=1, source_target_pairs={{0,32},{32,64},{64,96},{96,0},{1,33},{33,65},{65,97},{97,1},{2,34}... | collective-permute-start | bytes 245768 | tf_op jit(solution)/shard_map/ppermute | solution.py:377
  130.2 5.9 %collective-permute-start.6 = (f32[80,256]{1,0:T(8,128)S(1)}, f32[80,256]{1,0:T(8,128)S(1)}, u32[]{:S(2)}, u32[]{:S(2)}) collective-permute-start(f32[80,256]{1,0:T(8,128)S(1)} %convert_reduce_fusion), channel_id=1, source_target_pairs={{0,64},{32,96},{64,0},{96,32},{1,65},{33,97},{65,1},{97,33},{2,66}... | collective-permute-start | bytes 245768 | tf_op jit(solution)/shard_map/ppermute | solution.py:377
Sparse Core Ops, SparseCore 0:
  10.8 45.3 all-gather.1
where the time goes:
time: 145 us; the launch traced here: 144 us
  Pallas kernels  40.7 us (28%)
  waiting for transfers between devices  39.9 us (28%)
  starting transfers between devices  22.2 us (15%)
  blocking collectives  19 us (13%)
  between operations  14.1 us (10%)
  local copies, waits for them, and re-layouts  6.1 us (4%)
  other arithmetic  2.24 us (2%)
    pallas_call x1, Pallas kernels, backward(): pl.pallas_call(backward_kernel, out_shape=(jax.ShapeDtypeStruct((COLS, NO...  20.9 us
    all_to_all x1, blocking collectives, shards(): got = lax.all_to_all(sent, 'feat', 0, 0, tiled=True)  19 us
    pallas_call x1, Pallas kernels, forward(): pl.pallas_call(forward_kernel, out_shape=(jax.ShapeDtypeStruct((FEAT, 2 *...  16 us
    ppermute x9, starting transfers between devices, shift(): return lax.ppermute(value, 'dp', [(k, (k + by) % 4) for k in range(4)])  13.3 us
    all_to_all x1, waiting for transfers between devices, shards(): back = lax.all_to_all(back, 'feat', 0, 0, tiled=True)  11.8 us
    all_to_all x1, waiting for transfers between devices, shards(): wgrad = lax.all_to_all(wgrad, 'feat', 0, 0, tiled=True)  10.1 us
    ppermute x9, waiting for transfers between devices, shift(): return lax.ppermute(value, 'dp', [(k, (k + by) % 4) for k in range(4)])  9.59 us
    all_gather x1, waiting for transfers between devices, shards(): lax.all_gather(jnp.concatenate([self_weight, neigh_weight], axis=0), 'fea...  8.5 us
  transfers between devices with their start and end apart: 12, of which 9 were waited for; matrix products, arithmetic and copies ran while one was open for 1% of the time, Pallas kernels for 12%

commit v1 on v0

v1 whole, which is shorter than its diff:
```python
import jax
import jax.numpy as jnp
from jax import lax
from jax.experimental import pallas as pl
from jax.experimental.pallas import tpu as pltpu
from jax.sharding import PartitionSpec as P

BLK = 128
MAXB = 16
TB = 32
NBLK = 128
TGT = 4096
NODES = 16384
COLS = 32
FEAT = 32
WIDE = 256
CHUNK = 4
PER = MAXB // CHUNK
UNROLL = 8
LIST = TB * PER + UNROLL
MIB = 1024 * 1024

F32 = jnp.float32
BF16 = jnp.bfloat16
NT = (((1,), (1,)), ((), ()))


def dot(left, right):
    return jnp.dot(left, right, preferred_element_type=F32)


def dot_nt(left, right):
    return lax.dot_general(left, right, NT, preferred_element_type=F32)


def one_hot_rows(low_row):
    n = low_row.shape[1]
    rows = lax.broadcasted_iota(jnp.int32, (WIDE, n), 0)
    return jnp.where(rows == low_row, 1.0, 0.0).astype(BF16)


def list_chunks(cnt_ref, list_ref, tiles_ref, buf_ref, sem_ref):
    def fetch(chunk):
        span = pl.ds(chunk * CHUNK, CHUNK)
        return pltpu.make_async_copy(tiles_ref.at[span], buf_ref.at[span], sem_ref.at[chunk])

    def block(b, total):
        chunks = (cnt_ref[0, b] + (CHUNK - 1)) // CHUNK
        for k in range(PER):
            list_ref[total + k] = b * PER + k

            @pl.when(k < chunks)
            def _():
                fetch(b * PER + k).start()

        return total + chunks

    total = lax.fori_loop(0, TB, block, jnp.int32(0))
    for u in range(UNROLL):
        list_ref[total + u] = 0

    def wait():
        def body(i, carry):
            fetch(list_ref[i]).wait()
            return carry

        lax.fori_loop(0, total, body, 0)

    return total, wait


def chunk_slots(bid_ref, cnt_ref, list_ref, item, total):
    chunk = list_ref[item]
    block = chunk // PER
    first = (chunk % PER) * CHUNK
    count = jnp.where(item < total, cnt_ref[0, block], 0)
    slots = [(bid_ref[0, block, first + j], first + j < count) for j in range(CHUNK)]
    return chunk, block, slots


def place_marks(slot_ref, place_ref):
    slot = slot_ref[...]
    slot_lo = slot % WIDE
    for i in range(TGT // WIDE):
        span = slice(i * WIDE, (i + 1) * WIDE)
        place_ref[:, span] = one_hot_rows(slot_lo[:, span])
    return jnp.broadcast_to((slot // WIDE).astype(F32), (16, TGT)).astype(BF16)


def keep(values, high, wanted):
    mask = high == jnp.asarray(wanted, BF16)
    return [
        jnp.where(mask, values[r:r + 16], jnp.zeros((), BF16)) for r in range(0, values.shape[0], 16)
    ]


def forward_kernel(
    bid_ref, cnt_ref, feat_ref, tgt_ref, slot_ref, tiles_ref,
    out_ref, tgtq_ref,
    buf_ref, sem_ref, list_ref, place_ref, agg_ref,
):
    total, wait = list_chunks(cnt_ref, list_ref, tiles_ref, buf_ref, sem_ref)
    high16 = place_marks(slot_ref, place_ref)
    tgt = tgt_ref[...]
    row16 = lax.broadcasted_iota(jnp.int32, (16, TGT), 0)
    parts = jnp.where(row16 == 0, tgt // WIDE, jnp.where(row16 == 1, tgt % WIDE, 0)).astype(BF16)
    rows = []
    for q in range(TGT // WIDE):
        rows += keep(parts, high16, q)
    moved = dot_nt(jnp.concatenate(rows, axis=0), place_ref[...])
    for q in range(TGT // WIDE):
        tgtq_ref[:, q * WIDE:(q + 1) * WIDE] = moved[q * 16:q * 16 + 8]

    group = 32

    def gather(i, carry):
        span = pl.ds(pl.multiple_of(i * WIDE, WIDE), WIDE)
        ids = tgtq_ref[:, span]
        high = jnp.broadcast_to(ids[0:1], (8, WIDE))
        marks = one_hot_rows(ids[1:2].astype(jnp.int32))
        acc = [jnp.zeros((8, WIDE), F32) for _ in range(COLS // 8)]
        for g in range(NODES // WIDE // group):
            left = jnp.concatenate(
                [
                    feat_ref[:, (g * group + n) * WIDE:(g * group + n + 1) * WIDE]
                    for n in range(group)
                ],
                axis=0,
            )
            prod = dot(left, marks)
            for n in range(group):
                mask = high == float(g * group + n)
                for c in range(COLS // 8):
                    at = n * COLS + c * 8
                    acc[c] = jnp.where(mask, prod[at:at + 8], acc[c])
        own = jnp.concatenate(acc, axis=0).astype(BF16)
        out_ref[2 * i, :COLS] = own[:, :BLK]
        out_ref[2 * i + 1, :COLS] = own[:, BLK:]
        return carry

    lax.fori_loop(0, TGT // WIDE, gather, 0)

    agg_ref[...] = jnp.zeros_like(agg_ref)
    wait()

    def aggregate(i, carry):
        done = []
        for u in range(UNROLL):
            chunk, block, slots = chunk_slots(bid_ref, cnt_ref, list_ref, i * UNROLL + u, total)
            left = []
            for node_block, live in slots:
                span = pl.ds(pl.multiple_of(node_block * BLK, BLK), BLK)
                left.append(jnp.where(live, feat_ref[:, span], jnp.zeros((), BF16)))
            tiles = buf_ref[pl.ds(chunk * CHUNK, CHUNK)].reshape(CHUNK * BLK, BLK)
            done.append((block, dot(jnp.concatenate(left, axis=1), tiles)))
        for block, prod in done:
            span = pl.ds(pl.multiple_of(block * BLK, BLK), BLK)
            agg_ref[:, span] += prod
        return carry

    lax.fori_loop(0, (total + UNROLL - 1) // UNROLL, aggregate, 0)

    aggregate_rows = agg_ref[...].astype(BF16)
    half = 8
    for g in range(TGT // WIDE // half):
        rows = []
        for q in range(half):
            rows += keep(aggregate_rows, high16, g * half + q)
        moved = dot_nt(jnp.concatenate(rows, axis=0), place_ref[...]).astype(BF16)
        for q in range(half):
            piece = moved[q * COLS:(q + 1) * COLS]
            out_ref[2 * (g * half + q), COLS:] = piece[:, :BLK]
            out_ref[2 * (g * half + q) + 1, COLS:] = piece[:, BLK:]


VMEM = pl.BlockSpec(memory_space=pltpu.VMEM)
SMEM = pl.BlockSpec(memory_space=pltpu.SMEM)


HBM = pl.BlockSpec(memory_space=pl.ANY)


def params(mib):
    return pltpu.CompilerParams(vmem_limit_bytes=mib * MIB)


def cost(microseconds):
    return pl.CostEstimate(
        flops=microseconds * 1100 * MIB,
        bytes_accessed=int(microseconds * 3.5 * MIB),
        transcendentals=0,
    )


BLOCKS = jax.ShapeDtypeStruct((FEAT, 2 * COLS, BLK), BF16)
TILE_BUFFER = [
    pltpu.VMEM((TB * MAXB, BLK, BLK), BF16),
    pltpu.SemaphoreType.DMA((TB * PER,)),
    pltpu.SMEM((LIST,), jnp.int32),
]


def forward(block_ids, counts, features, targets, slots, tiles):
    return pl.pallas_call(
        forward_kernel,
        out_shape=(
            BLOCKS,
            jax.ShapeDtypeStruct((8, TGT), F32),
        ),
        in_specs=[SMEM, SMEM, VMEM, VMEM, VMEM, HBM],
        out_specs=(VMEM, VMEM),
        scratch_shapes=TILE_BUFFER
        + [pltpu.VMEM((WIDE, TGT), BF16), pltpu.VMEM((COLS, TGT), F32)],
        compiler_params=params(40),
        cost_estimate=cost(15),
        name="gather_and_aggregate",
    )(block_ids, counts, features, targets, slots, tiles)


def middle_kernel(
    x_ref, w_ref, bias_ref, grad_ref, hidden_ref, back_ref, wgrad_ref
):
    half = FEAT * COLS
    x_own = x_ref[:, :COLS].reshape(half, BLK)
    x_agg = x_ref[:, COLS:].reshape(half, BLK)
    w_own = w_ref[:, :COLS].reshape(half, WIDE)
    w_agg = w_ref[:, COLS:].reshape(half, WIDE)
    tn = (((0,), (0,)), ((), ()))
    preact = lax.dot_general(x_own, w_own, tn, preferred_element_type=F32)
    preact = preact + lax.dot_general(x_agg, w_agg, tn, preferred_element_type=F32)
    preact = preact + bias_ref[...]
    sig = jax.nn.sigmoid(preact)
    hidden_ref[0] = (preact * sig).astype(BF16)
    slope = (grad_ref[0].astype(F32) * sig * (1.0 + preact * (1.0 - sig))).astype(BF16)
    back_ref[:, :COLS] = dot_nt(w_own, slope).astype(BF16).reshape(FEAT, COLS, BLK)
    back_ref[:, COLS:] = dot_nt(w_agg, slope).astype(BF16).reshape(FEAT, COLS, BLK)
    wgrad_ref[:, :COLS] = dot(x_own, slope).astype(BF16).reshape(FEAT, COLS, WIDE)
    wgrad_ref[:, COLS:2 * COLS] = dot(x_agg, slope).astype(BF16).reshape(FEAT, COLS, WIDE)
    total = jnp.sum(slope.astype(F32), axis=0, keepdims=True)
    first = total.astype(BF16).astype(F32)
    rest = total - first
    second = rest.astype(BF16).astype(F32)
    third = rest - second
    row = lax.broadcasted_iota(jnp.int32, (16, WIDE), 0)
    tail = jnp.where(
        row == 0, first, jnp.where(row == 1, second, jnp.where(row == 2, third, 0.0))
    ).astype(BF16)
    wgrad_ref[:, 2 * COLS:] = jnp.broadcast_to(tail[None], (FEAT, 16, WIDE))


def middle(x, w, bias, grad):
    return pl.pallas_call(
        middle_kernel,
        out_shape=(
            jax.ShapeDtypeStruct((1, BLK, WIDE), BF16),
            BLOCKS,
            jax.ShapeDtypeStruct((FEAT, 2 * COLS + 16, WIDE), BF16),
        ),
        in_specs=[VMEM] * 4,
        out_specs=(VMEM,) * 3,
        compiler_params=params(24),
        cost_estimate=cost(2),
        name="hidden_and_slope",
    )(x, w, bias, grad)


def spread_kernel(
    bid_ref, cnt_ref, back_ref, slot_ref, tiles_ref, grad_ref, buf_ref, sem_ref, list_ref, rows_ref
):
    total, wait = list_chunks(cnt_ref, list_ref, tiles_ref, buf_ref, sem_ref)
    slot = slot_ref[...]
    slot_hi = (slot // WIDE).astype(F32)
    slot_lo = slot % WIDE
    pairs = TGT // WIDE
    left = jnp.concatenate(
        [jnp.concatenate([back_ref[2 * q, COLS:], back_ref[2 * q + 1, COLS:]], axis=1) for q in range(pairs)],
        axis=0,
    )
    for i in range(TGT // WIDE):
        span = slice(i * WIDE, (i + 1) * WIDE)
        prod = dot(left, one_hot_rows(slot_lo[:, span]))
        high = jnp.broadcast_to(slot_hi[:, span], (8, WIDE))
        acc = [jnp.zeros((8, WIDE), F32) for _ in range(COLS // 8)]
        for q in range(pairs):
            mask = high == float(q)
            for c in range(COLS // 8):
                at = q * COLS + c * 8
                acc[c] = jnp.where(mask, prod[at:at + 8], acc[c])
        rows_ref[:, span] = jnp.concatenate(acc, axis=0).astype(BF16)

    grad_ref[...] = jnp.zeros_like(grad_ref)
    wait()

    def spread(i, carry):
        done = []
        for u in range(UNROLL):
            chunk, block, slots = chunk_slots(bid_ref, cnt_ref, list_ref, i * UNROLL + u, total)
            span = pl.ds(pl.multiple_of(block * BLK, BLK), BLK)
            tiles = buf_ref[pl.ds(chunk * CHUNK, CHUNK)].reshape(CHUNK * BLK, BLK)
            done.append((slots, dot_nt(rows_ref[:, span], tiles)))
        for slots, prod in done:
            for j, (node_block, live) in enumerate(slots):
                piece = prod[:, j * BLK:(j + 1) * BLK]
                span = pl.ds(pl.multiple_of(node_block * BLK, BLK), BLK)
                grad_ref[:, span] += jnp.where(live, piece, 0.0)
        return carry

    lax.fori_loop(0, (total + UNROLL - 1) // UNROLL, spread, 0)


def spread_part(block_ids, counts, back, slots, tiles):
    return pl.pallas_call(
        spread_kernel,
        out_shape=jax.ShapeDtypeStruct((COLS, NODES), F32),
        in_specs=[SMEM, SMEM, VMEM, VMEM, HBM],
        out_specs=VMEM,
        scratch_shapes=TILE_BUFFER + [pltpu.VMEM((COLS, TGT), BF16)],
        compiler_params=params(40),
        cost_estimate=cost(7),
        name="spread",
    )(block_ids, counts, back, slots, tiles)


QUARTER = NODES // 4


def scatter_kernel(zid_ref, grad_ref, back_ref, tgtq_ref, *refs, steps):
    out_refs, mark_ref = refs[:-1], refs[-1]
    ids = tgtq_ref[...]
    for i in range(TGT // WIDE):
        span = slice(i * WIDE, (i + 1) * WIDE)
        mark_ref[:, span] = one_hot_rows(ids[1:2, span].astype(jnp.int32))
    high16 = jnp.broadcast_to(ids[0:1], (16, TGT)).astype(BF16)
    own = jnp.concatenate([back_ref[q, :COLS] for q in range(FEAT)], axis=1)
    per = QUARTER // WIDE
    half = 8
    for step, out_ref in zip(steps, out_refs):
        which = lax.rem(zid_ref[0] + step, 4)
        for g in range(per // half):
            rows = []
            for n in range(half):
                wanted = (which * per + g * half + n).astype(F32).astype(BF16)
                rows += keep(own, high16, wanted)
            prod = dot_nt(jnp.concatenate(rows, axis=0), mark_ref[...])
            for n in range(half):
                at = (g * half + n) * WIDE
                span = pl.ds(pl.multiple_of(which * QUARTER + at, WIDE), WIDE)
                value = grad_ref[:, span] + prod[n * COLS:(n + 1) * COLS]
                out_ref[:, at:at + WIDE] = value.astype(out_ref.dtype)


def scatter_part(zid, grad, back, tgtq, steps):
    return pl.pallas_call(
        lambda *refs: scatter_kernel(*refs, steps=steps),
        out_shape=tuple(
            jax.ShapeDtypeStruct((COLS, QUARTER), BF16 if step else F32) for step in steps
        ),
        in_specs=[SMEM, VMEM, VMEM, VMEM],
        out_specs=tuple(VMEM for _ in steps),
        scratch_shapes=[pltpu.VMEM((WIDE, TGT), BF16)],
        compiler_params=params(24),
        cost_estimate=cost(1 + len(steps)),
        name="scatter",
    )(zid, grad, back, tgtq)


def place_kernel(zid_ref, a_ref, b_ref, c_ref, d_ref, out_ref):
    quarter = NODES // 4
    for step, ref in enumerate((a_ref, b_ref, c_ref, d_ref)):
        at = pl.multiple_of(lax.rem(zid_ref[0] + step, 4) * quarter, quarter)
        out_ref[:, pl.ds(at, quarter)] = ref[...].astype(F32)


def place(zid, quarters):
    return pl.pallas_call(
        place_kernel,
        out_shape=jax.ShapeDtypeStruct((COLS, NODES), F32),
        in_specs=[SMEM] + [VMEM] * 4,
        out_specs=VMEM,
        compiler_params=params(32),
        cost_estimate=cost(1),
        name="place_quarters",
    )(zid, *quarters)


def shift(value, by):
    return lax.ppermute(value, "dp", [(k, (k + by) % 4) for k in range(4)])


def relay(value):
    pairs = [
        (k * FEAT + f, ((k + (1 if f % 2 == 0 else 3)) % 4) * FEAT + f)
        for k in range(4)
        for f in range(FEAT)
    ]
    return lax.ppermute(value, ("dp", "feat"), pairs)


def exchange(value):
    return lax.all_to_all(value, "feat", 0, 0, tiled=True)


def shards(
    features,
    targets,
    block_ids,
    counts,
    target_slots,
    edge_tiles,
    self_weight,
    neigh_weight,
    hidden_bias,
    hidden_grad,
):
    tiles = edge_tiles.reshape(TB * MAXB, BLK, BLK)
    zid = lax.axis_index("dp").astype(jnp.int32).reshape(1)

    side = lax.axis_index("feat") % 2

    weights = jnp.concatenate([self_weight, neigh_weight], axis=0)
    weights = exchange(jnp.broadcast_to(weights[None], (FEAT, 2 * COLS, WIDE)))
    sent, tgtq = forward(block_ids, counts, features, targets, target_slots, tiles)
    sent, weights = lax.optimization_barrier((sent, weights))
    hidden, back, wgrad = middle(
        exchange(sent), weights, hidden_bias.reshape(1, -1), hidden_grad
    )
    back = exchange(back)
    grad = spread_part(block_ids, counts, back, target_slots, tiles)
    (far2,) = scatter_part(zid, grad, back, tgtq, (2,))
    grad, far2 = lax.optimization_barrier((grad, far2))
    far1, far3 = scatter_part(zid, grad, back, tgtq, (1, 3))
    grad, far1, far3, wgrad = lax.optimization_barrier((grad, far1, far3, wgrad))
    (near,) = scatter_part(zid, grad, back, tgtq, (0,))

    relayed = relay(far2)
    to_next = far1.astype(F32) + jnp.where(side == 0, relayed, 0).astype(F32)
    to_last = far3.astype(F32) + jnp.where(side == 1, relayed, 0).astype(F32)
    from_last, from_next = shift(to_next.astype(BF16), 1), shift(to_last.astype(BF16), 3)

    wgrad = exchange(wgrad)
    wsum = jnp.sum(wgrad.astype(F32), axis=0)
    wsum = (wsum + shift(wsum, 2)) + (shift(wsum, 1) + shift(wsum, 3))
    self_grad = wsum[:COLS]
    neigh_grad = wsum[COLS:2 * COLS]
    bias_grad = wsum[2 * COLS] + (wsum[2 * COLS + 1] + wsum[2 * COLS + 2])

    done = (near + from_last.astype(F32) + from_next.astype(F32)).astype(BF16)
    of_last, of_next = shift(done, 1), shift(done, 3)
    of_far = relay(jnp.where(side == 0, of_last, of_next))
    feature_grad = place(zid, (done, of_next, of_far, of_last))
    return (hidden, feature_grad, self_grad, neigh_grad, bias_grad)


def solution(mesh):
    return jax.shard_map(
        shards,
        mesh=mesh,
        in_specs=(
            P("feat", None),
            P("dp", None),
            P("dp", None, None),
            P("dp", None),
            P("dp", None),
            P("dp", None, None, None, None),
            P("feat", None),
            P("feat", None),
            P(),
            P("dp", "feat", None),
        ),
        out_specs=(P("dp", "feat", None), P("feat", None), P("feat", None), P("feat", None), P()),
        check_vma=False,
    )
```

time: 145 us -> 125 us (0.86)
  between operations: 14.1 us -> 0.89 us
  Pallas kernels: 40.7 us -> 36.4 us
  local copies, waits for them, and re-layouts: 6.1 us -> 1.84 us
  starting transfers between devices: 22.2 us -> 24.9 us
  waiting for transfers between devices: 39.9 us -> 37.5 us
  other arithmetic: 2.24 us -> 3.99 us
    all_gather x1 -> x0, waiting for transfers between devices: 8.5 us -> none  [shards(): lax.all_gather(jnp.concatenate([self_weight, neigh_weight], axis=0), 'fea...]
    all_to_all x2 -> x3, starting transfers between devices: 8.87 us -> 16.2 us  [exchange(): return lax.all_to_all(value, 'feat', 0, 0, tiled=True)]
    unnamed x19, local copies, waits for them, and re-layouts: 5.34 us -> 0.12 us
    ppermute x0 -> x2, waiting for transfers between devices: none -> 5.16 us  [relay(): return lax.ppermute(value, ('dp', 'feat'), pairs)]
    ppermute x9 -> x7, starting transfers between devices: 13.3 us -> 8.62 us  [shift(): return lax.ppermute(value, 'dp', [(k, (k + by) % 4) for k in range(4)])]
    pallas_call x3 -> x6, Pallas kernels: 39.2 us -> 34.9 us  [the longest x1 16.8 us: forward(): pl.pallas_call(forward_kernel, out_shape=(BLOCKS, jax.ShapeDtypeStruct((8...]
    ppermute x9 -> x7, waiting for transfers between devices: 9.59 us -> 10.6 us  [shift(): return lax.ppermute(value, 'dp', [(k, (k + by) % 4) for k in range(4)])]
    all_to_all x2 -> x3, waiting for transfers between devices: 21.8 us -> 21.8 us  [exchange(): return lax.all_to_all(value, 'feat', 0, 0, tiled=True)]
  transfers between devices with their start and end apart: 12 -> 12, of which waited for: 9 -> 8; matrix products, arithmetic and copies ran while one was open for 1% -> 1% of each run, Pallas kernels for 12% -> 18%
where the time goes in v1:
time: 125 us; the launch traced here: 124 us
  waiting for transfers between devices  37.5 us (30%)
  Pallas kernels  36.4 us (29%)
  starting transfers between devices  24.9 us (20%)
  blocking collectives  18.6 us (15%)
  other arithmetic  3.99 us (3%)
  local copies, waits for them, and re-layouts  1.84 us (1%)
    all_to_all x3, waiting for transfers between devices, exchange(): return lax.all_to_all(value, 'feat', 0, 0, tiled=True)  21.8 us
    all_to_all x1, blocking collectives, exchange(): return lax.all_to_all(value, 'feat', 0, 0, tiled=True)  18.6 us
    pallas_call x1, Pallas kernels, forward(): pl.pallas_call(forward_kernel, out_shape=(BLOCKS, jax.ShapeDtypeStruct((8...  16.8 us
    all_to_all x3, starting transfers between devices, exchange(): return lax.all_to_all(value, 'feat', 0, 0, tiled=True)  16.2 us
    pallas_call x1, Pallas kernels, spread_part(): pl.pallas_call(spread_kernel, out_shape=jax.ShapeDtypeStruct((COLS, NODES...  10.7 us
    ppermute x7, waiting for transfers between devices, shift(): return lax.ppermute(value, 'dp', [(k, (k + by) % 4) for k in range(4)])  10.6 us
    ppermute x7, starting transfers between devices, shift(): return lax.ppermute(value, 'dp', [(k, (k + by) % 4) for k in range(4)])  8.62 us
    ppermute x2, waiting for transfers between devices, relay(): return lax.ppermute(value, ('dp', 'feat'), pairs)  5.16 us
  transfers between devices with their start and end apart: 12, of which 8 were waited for; matrix products, arithmetic and copies ran while one was open for 1% of the time, Pallas kernels for 18%

profile of v1, /device:TPU:0, one launch (start us, length us, event | category | flops | bytes accessed | tf_op | source)
XLA Modules:
  0.0 124.1 jit_solution(11151908468260443788)
XLA Ops:
  0.7 0.8 pad_maximum_fusion
  1.5 1.1 broadcast_in_dim.11
  2.6 7.4 %all-to-all-start = ((bf16[32,64,256]{2,1,0:T(8,128)(2,1)}), bf16[32,64,256]{2,1,0:T(8,128)(2,1)S(1)}, u32[]{:S(2)}, u32[]{:S(2)}) async-start(bf16[32,64,256]{2,1,0:T(8,128)(2,1)} %broadcast_in_dim.11), calls=%async_computation | async-start | bytes 2097152 | tf_op jit(solution)/shard_map/all_to_all | solution.py:400
  10.1 16.8 %gather_and_aggregate.1 = (bf16[32,64,128]{2,1,0:T(8,128)(2,1)S(1)}, f32[8,4096]{1,0:T(8,128)S(1)}) custom-call(s32[1,32,16]{2,1,0:T(8,128)S(1)} %copy.15.bid_ref, s32[1,32]{1,0:T(1,128)S(1)} %copy-done.5, bf16[32,16384]{1,0:T(8,128)(2,1)S(1)} %copy-done, s32[1,4096]{1,0:T(1,128)S(1)} %copy-done.2, s32[1,4096]{1,0:T(1,128)S(1)} %copy-done.3, ...), custom_call_target="tpu_custom_call" | custom-call | flops 17301504000 | bytes 55050240 | tf_op jit(solution)/shard_map/gather_and_aggregate/pallas_call | solution.py:204
  27.0 0.4 all-to-all-done.w_ref
  27.3 18.6 %all_to_all.20.x_ref = bf16[32,64,128]{2,1,0:T(8,128)(2,1)S(1)} all-to-all(bf16[32,64,128]{2,1,0:T(8,128)(2,1)S(1)} %get-tuple-element.21), channel_id=1, replica_groups=mesh['dp'=4,'feat'=32] {'feat'}, dimensions={0} | all-to-all | bytes 1048576 | tf_op jit(solution)/shard_map/all_to_all | solution.py:400
  46.0 2.4 %hidden_and_slope.1 = (bf16[1,128,256]{2,1,0:T(8,128)(2,1)}, bf16[32,64,128]{2,1,0:T(8,128)(2,1)}, bf16[32,80,256]{2,1,0:T(8,128)(2,1)}) custom-call(bf16[32,64,128]{2,1,0:T(8,128)(2,1)S(1)} %all_to_all.20.x_ref, bf16[32,64,256]{2,1,0:T(8,128)(2,1)S(1)} %all-to-all-done.w_ref, f32[1,256]{1,0:T(1,128)S(1)} %bitcast.4, bf16[1,128,256]{2,1,0:T(8,128)(2,1)S(1)} %copy-done.1), custom_call_target="tpu_custom_call" | custom-call | flops 2306867200 | bytes 7340032 | tf_op jit(solution)/shard_map/hidden_and_slope/pallas_call | solution.py:252
  48.3 3.9 %all-to-all-start.2 = ((bf16[32,64,128]{2,1,0:T(8,128)(2,1)}), bf16[32,64,128]{2,1,0:T(8,128)(2,1)S(1)}, u32[]{:S(2)}, u32[]{:S(2)}) async-start(bf16[32,64,128]{2,1,0:T(8,128)(2,1)} %get-tuple-element.24), calls=%async_computation.2 | async-start | bytes 1048576 | tf_op jit(solution)/shard_map/all_to_all | solution.py:400
  52.2 11.7 %all-to-all-done.2.back_ref.refs_2_ = bf16[32,64,128]{2,1,0:T(8,128)(2,1)S(1)} async-done(((bf16[32,64,128]{2,1,0:T(8,128)(2,1)}), bf16[32,64,128]{2,1,0:T(8,128)(2,1)S(1)}, u32[]{:S(2)}, u32[]{:S(2)}) %all-to-all-start.2) | async-done | bytes 524320 | tf_op jit(solution)/shard_map/all_to_all | solution.py:400
  64.0 10.7 %spread.1.refs_1_ = f32[32,16384]{1,0:T(8,128)S(1)} custom-call(s32[1,32,16]{2,1,0:T(8,128)S(1)} %copy.15.bid_ref, s32[1,32]{1,0:T(1,128)S(1)} %copy-done.5, bf16[32,64,128]{2,1,0:T(8,128)(2,1)S(1)} %all-to-all-done.2.back_ref.refs_2_, s32[1,4096]{1,0:T(1,128)S(1)} %copy-done.3, bf16[512,128,128]{2,1,0:T(8,128)(2,1)} %bitcast.7), custom_call_target="tpu_custom_call" | custom-call | flops 8074035200 | bytes 25690112 | tf_op jit(solution)/shard_map/spread/pallas_call | solution.py:312
  74.8 1.3 %scatter.3 = bf16[32,4096]{1,0:T(8,128)(2,1)S(1)} custom-call(s32[1]{0:T(128)} %bitcast.2.refs_0_.zid_ref, f32[32,16384]{1,0:T(8,128)S(1)} %spread.1.refs_1_, bf16[32,64,128]{2,1,0:T(8,128)(2,1)S(1)} %all-to-all-done.2.back_ref.refs_2_, f32[8,4096]{1,0:T(8,128)S(1)} %get-tuple-element.25.refs_3_), custom_call_target="tpu_custom_call" | custom-call | flops 2306867200 | bytes 7340032 | tf_op jit(solution)/shard_map/scatter/pallas_call | solution.py:353
  76.0 0.1 collective-permute-start
  76.1 2.4 %scatter.4 = (bf16[32,4096]{1,0:T(8,128)(2,1)S(1)}, bf16[32,4096]{1,0:T(8,128)(2,1)S(1)}) custom-call(s32[1]{0:T(128)} %bitcast.2.refs_0_.zid_ref, f32[32,16384]{1,0:T(8,128)S(1)} %spread.1.refs_1_, bf16[32,64,128]{2,1,0:T(8,128)(2,1)S(1)} %all-to-all-done.2.back_ref.refs_2_, f32[8,4096]{1,0:T(8,128)S(1)} %get-tuple-element.25.refs_3_), custom_call_target="tpu_custom_call" | custom-call | flops 3460300800 | bytes 11010048 | tf_op jit(solution)/shard_map/scatter/pallas_call | solution.py:353
  78.5 5.2 %collective-permute-done = bf16[32,4096]{1,0:T(8,128)(2,1)S(1)} collective-permute-done((bf16[32,4096]{1,0:T(8,128)(2,1)S(1)}, bf16[32,4096]{1,0:T(8,128)(2,1)S(1)}, u32[]{:S(2)}, u32[]{:S(2)}) %collective-permute-start) | collective-permute-done | bytes 262176 | tf_op jit(solution)/shard_map/ppermute | solution.py:396
  83.7 0.9 add_convert_fusion.2
  84.6 3.2 %collective-permute-start.2 = (bf16[32,4096]{1,0:T(8,128)(2,1)}, bf16[32,4096]{1,0:T(8,128)(2,1)S(1)}, u32[]{:S(2)}, u32[]{:S(2)}) collective-permute-start(bf16[32,4096]{1,0:T(8,128)(2,1)} %get-tuple-element.36), channel_id=1, source_target_pairs={{0,96},{32,0},{64,32},{96,64},{1,97},{33,1},{65,33},{97,65},{2,98}... | collective-permute-start | bytes 786440 | tf_op jit(solution)/shard_map/ppermute | solution.py:387
  87.9 4.9 %all-to-all-start.3 = ((bf16[32,80,256]{2,1,0:T(8,128)(2,1)}), bf16[32,80,256]{2,1,0:T(8,128)(2,1)}, u32[]{:S(2)}, u32[]{:S(2)}) async-start(bf16[32,80,256]{2,1,0:T(8,128)(2,1)} %get-tuple-element.34), calls=%async_computation.3 | async-start | bytes 2621440 | tf_op jit(solution)/shard_map/all_to_all | solution.py:400
  92.8 1.3 %scatter.5 = f32[32,4096]{1,0:T(8,128)S(1)} custom-call(s32[1]{0:T(128)} %bitcast.2.refs_0_.zid_ref, f32[32,16384]{1,0:T(8,128)S(1)} %copy-done.7, bf16[32,64,128]{2,1,0:T(8,128)(2,1)S(1)} %all-to-all-done.2.back_ref.refs_2_, f32[8,4096]{1,0:T(8,128)S(1)} %get-tuple-element.25.refs_3_), custom_call_target="tpu_custom_call" | custom-call | flops 2306867200 | bytes 7340032 | tf_op jit(solution)/shard_map/scatter/pallas_call | solution.py:353
  94.1 0.1 add_convert_fusion.a_ref
  94.2 0.1 collective-permute-start.4
  94.2 3.2 %collective-permute-start.3 = (bf16[32,4096]{1,0:T(8,128)(2,1)S(1)}, bf16[32,4096]{1,0:T(8,128)(2,1)S(1)}, u32[]{:S(2)}, u32[]{:S(2)}) collective-permute-start(bf16[32,4096]{1,0:T(8,128)(2,1)S(1)} %add_convert_fusion.a_ref), channel_id=1, source_target_pairs={{0,96},{32,0},{64,32},{96,64},{1,97},{33,1},{65,33},{97,65},{2,98}... | collective-permute-start | bytes 786440 | tf_op jit(solution)/shard_map/ppermute | solution.py:387
  97.5 6.1 %collective-permute-done.4.d_ref = bf16[32,4096]{1,0:T(8,128)(2,1)S(1)} collective-permute-done((bf16[32,4096]{1,0:T(8,128)(2,1)S(1)}, bf16[32,4096]{1,0:T(8,128)(2,1)S(1)}, u32[]{:S(2)}, u32[]{:S(2)}) %collective-permute-start.4) | collective-permute-done | bytes 262176 | tf_op jit(solution)/shard_map/ppermute | solution.py:387
  103.6 0.1 collective-permute-start.5
  103.7 9.6 %all-to-all-done.3 = bf16[32,80,256]{2,1,0:T(8,128)(2,1)} async-done(((bf16[32,80,256]{2,1,0:T(8,128)(2,1)}), bf16[32,80,256]{2,1,0:T(8,128)(2,1)}, u32[]{:S(2)}, u32[]{:S(2)}) %all-to-all-start.3) | async-done | bytes 1310752 | tf_op jit(solution)/shard_map/all_to_all | solution.py:400
  113.4 1.5 %convert_reduce_fusion = f32[80,256]{1,0:T(8,128)S(1)} fusion(bf16[32,80,256]{2,1,0:T(8,128)(2,1)} %all-to-all-done.3), kind=kLoop, calls=%fused_computation | loop fusion | flops 1290240 | bytes 1392640 | tf_op jit(solution)/shard_map/reduce_sum | solution.py:441
  114.9 2.0 %collective-permute-start.7 = (f32[80,256]{1,0:T(8,128)S(1)}, f32[80,256]{1,0:T(8,128)S(1)}, u32[]{:S(2)}, u32[]{:S(2)}) collective-permute-start(f32[80,256]{1,0:T(8,128)S(1)} %convert_reduce_fusion), channel_id=1, source_target_pairs={{0,32},{32,64},{64,96},{96,0},{1,33},{33,65},{65,97},{97,1},{2,34}... | collective-permute-start | bytes 245768 | tf_op jit(solution)/shard_map/ppermute | solution.py:387
  117.0 1.5 %place_quarters.1 = f32[32,16384]{1,0:T(8,128)} custom-call(s32[1]{0:T(128)} %bitcast.2.refs_0_.zid_ref, bf16[32,4096]{1,0:T(8,128)(2,1)S(1)} %add_convert_fusion.a_ref, bf16[32,4096]{1,0:T(8,128)(2,1)S(1)} %collective-permute-done.3.b_ref, bf16[32,4096]{1,0:T(8,128)(2,1)S(1)} %collective-permute-done.5.c_ref, bf16[32,4096]{1,0:T(8,128)(2,1)S(1)} %collective-permute-done.4.d_ref), custom_call_target="tpu_custom_call" | custom-call | flops 1153433600 | bytes 3670016 | tf_op jit(solution)/shard_map/place_quarters/pallas_call | solution.py:375
  118.4 1.3 %collective-permute-done.8 = f32[80,256]{1,0:T(8,128)S(1)} collective-permute-done((f32[80,256]{1,0:T(8,128)S(1)}, f32[80,256]{1,0:T(8,128)S(1)}, u32[]{:S(2)}, u32[]{:S(2)}) %collective-permute-start.8) | collective-permute-done | bytes 81952 | tf_op jit(solution)/shard_map/ppermute | solution.py:387
  119.7 1.1 collective-permute-done.7
  120.8 2.1 %collective-permute-done.6 = f32[80,256]{1,0:T(8,128)S(1)} collective-permute-done((f32[80,256]{1,0:T(8,128)S(1)}, f32[80,256]{1,0:T(8,128)S(1)}, u32[]{:S(2)}, u32[]{:S(2)}) %collective-permute-start.6) | collective-permute-done | bytes 81952 | tf_op jit(solution)/shard_map/ppermute | solution.py:387
  122.9 0.6 fusion
  123.5 0.6 fusion.1
  (28 shorter events, 0.3 us)
Async XLA Ops:
  0.6 9.4 %copy-start.8 = (s32[1,32,16]{1,2,0:T(8,128)S(1)}, s32[1,32,16]{1,2,0:T(8,128)}, u32[]{:S(2)}) copy-start(s32[1,32,16]{1,2,0:T(8,128)} %param.12) | copy-start | bytes 6148
  0.6 9.5 %copy-start.3 = (s32[1,4096]{1,0:T(1,128)S(1)}, s32[1,4096]{1,0:T(1,128)}, u32[]{:S(2)}) copy-start(s32[1,4096]{1,0:T(1,128)} %slot_ref.3) | copy-start | bytes 49156
  0.7 9.4 %copy-start.5 = (s32[1,32]{1,0:T(1,128)S(1)}, s32[1,32]{1,0:T(1,128)}, u32[]{:S(2)}) copy-start(s32[1,32]{1,0:T(1,128)} %cnt_ref.3) | copy-start | bytes 388
  0.7 9.4 %copy-start.2 = (s32[1,4096]{1,0:T(1,128)S(1)}, s32[1,4096]{1,0:T(1,128)}, u32[]{:S(2)}) copy-start(s32[1,4096]{1,0:T(1,128)} %tgt_ref.1) | copy-start | bytes 49156
  0.7 9.4 %copy-start = (bf16[32,16384]{1,0:T(8,128)(2,1)S(1)}, bf16[32,16384]{1,0:T(8,128)(2,1)}, u32[]{:S(2)}) copy-start(bf16[32,16384]{1,0:T(8,128)(2,1)} %feat_ref.1) | copy-start | bytes 3145732
  2.6 24.7 %all-to-all-start = ((bf16[32,64,256]{2,1,0:T(8,128)(2,1)}), bf16[32,64,256]{2,1,0:T(8,128)(2,1)S(1)}, u32[]{:S(2)}, u32[]{:S(2)}) async-start(bf16[32,64,256]{2,1,0:T(8,128)(2,1)} %broadcast_in_dim.11), calls=%async_computation | async-start | bytes 2097152 | tf_op jit(solution)/shard_map/all_to_all | solution.py:400
  10.1 35.8 %copy-start.1 = (bf16[1,128,256]{2,1,0:T(8,128)(2,1)S(1)}, bf16[1,128,256]{2,1,0:T(8,128)(2,1)}, u32[]{:S(2)}) copy-start(bf16[1,128,256]{2,1,0:T(8,128)(2,1)} %grad_ref.1) | copy-start | bytes 196612
  10.1 35.8 %copy-start.4 = (f32[256]{0:T(256)S(1)}, f32[256]{0:T(256)}, u32[]{:S(2)}) copy-start(f32[256]{0:T(256)} %param.18) | copy-start | bytes 3076
  48.3 15.7 %all-to-all-start.2 = ((bf16[32,64,128]{2,1,0:T(8,128)(2,1)}), bf16[32,64,128]{2,1,0:T(8,128)(2,1)S(1)}, u32[]{:S(2)}, u32[]{:S(2)}) async-start(bf16[32,64,128]{2,1,0:T(8,128)(2,1)} %get-tuple-element.24), calls=%async_computation.2 | async-start | bytes 1048576 | tf_op jit(solution)/shard_map/all_to_all | solution.py:400
  74.7 1.4 %copy-start.6 = (f32[32,16384]{1,0:T(8,128)}, f32[32,16384]{1,0:T(8,128)S(1)}, u32[]{:S(2)}) copy-start(f32[32,16384]{1,0:T(8,128)S(1)} %spread.1.refs_1_) | copy-start | bytes 6291460
  76.0 7.7 %collective-permute-start = (bf16[32,4096]{1,0:T(8,128)(2,1)S(1)}, bf16[32,4096]{1,0:T(8,128)(2,1)S(1)}, u32[]{:S(2)}, u32[]{:S(2)}) collective-permute-start(bf16[32,4096]{1,0:T(8,128)(2,1)S(1)} %scatter.3), channel_id=1, source_target_pairs={{0,32},{1,97},{2,34},{3,99},{4,36},{5,101},{6,38},{7,103},{8,40},{... | collective-permute-start | bytes 786440 | tf_op jit(solution)/shard_map/ppermute | solution.py:396
  78.5 14.2 %copy-start.7 = (f32[32,16384]{1,0:T(8,128)S(1)}, f32[32,16384]{1,0:T(8,128)}, u32[]{:S(2)}) copy-start(f32[32,16384]{1,0:T(8,128)} %copy-done.6) | copy-start | bytes 6291460
  84.6 9.4 %collective-permute-start.1 = (bf16[32,4096]{1,0:T(8,128)(2,1)}, bf16[32,4096]{1,0:T(8,128)(2,1)S(1)}, u32[]{:S(2)}, u32[]{:S(2)}) collective-permute-start(bf16[32,4096]{1,0:T(8,128)(2,1)} %get-tuple-element.35), channel_id=1, source_target_pairs={{0,32},{32,64},{64,96},{96,0},{1,33},{33,65},{65,97},{97,1},{2,34}... | collective-permute-start | bytes 786440 | tf_op jit(solution)/shard_map/ppermute | solution.py:387
  84.6 9.4 %collective-permute-start.2 = (bf16[32,4096]{1,0:T(8,128)(2,1)}, bf16[32,4096]{1,0:T(8,128)(2,1)S(1)}, u32[]{:S(2)}, u32[]{:S(2)}) collective-permute-start(bf16[32,4096]{1,0:T(8,128)(2,1)} %get-tuple-element.36), channel_id=1, source_target_pairs={{0,96},{32,0},{64,32},{96,64},{1,97},{33,1},{65,33},{97,65},{2,98}... | collective-permute-start | bytes 786440 | tf_op jit(solution)/shard_map/ppermute | solution.py:387
  87.9 25.5 %all-to-all-start.3 = ((bf16[32,80,256]{2,1,0:T(8,128)(2,1)}), bf16[32,80,256]{2,1,0:T(8,128)(2,1)}, u32[]{:S(2)}, u32[]{:S(2)}) async-start(bf16[32,80,256]{2,1,0:T(8,128)(2,1)} %get-tuple-element.34), calls=%async_computation.3 | async-start | bytes 2621440 | tf_op jit(solution)/shard_map/all_to_all | solution.py:400
  94.2 9.4 %collective-permute-start.4 = (bf16[32,4096]{1,0:T(8,128)(2,1)S(1)}, bf16[32,4096]{1,0:T(8,128)(2,1)S(1)}, u32[]{:S(2)}, u32[]{:S(2)}) collective-permute-start(bf16[32,4096]{1,0:T(8,128)(2,1)S(1)} %add_convert_fusion.a_ref), channel_id=1, source_target_pairs={{0,32},{32,64},{64,96},{96,0},{1,33},{33,65},{65,97},{97,1},{2,34}... | collective-permute-start | bytes 786440 | tf_op jit(solution)/shard_map/ppermute | solution.py:387
  94.2 9.3 %collective-permute-start.3 = (bf16[32,4096]{1,0:T(8,128)(2,1)S(1)}, bf16[32,4096]{1,0:T(8,128)(2,1)S(1)}, u32[]{:S(2)}, u32[]{:S(2)}) collective-permute-start(bf16[32,4096]{1,0:T(8,128)(2,1)S(1)} %add_convert_fusion.a_ref), channel_id=1, source_target_pairs={{0,96},{32,0},{64,32},{96,64},{1,97},{33,1},{65,33},{97,65},{2,98}... | collective-permute-start | bytes 786440 | tf_op jit(solution)/shard_map/ppermute | solution.py:387
  103.6 13.3 %collective-permute-start.5 = (bf16[32,4096]{1,0:T(8,128)(2,1)S(1)}, bf16[32,4096]{1,0:T(8,128)(2,1)S(1)}, u32[]{:S(2)}, u32[]{:S(2)}) collective-permute-start(bf16[32,4096]{1,0:T(8,128)(2,1)S(1)} %broadcast_select_fusion), channel_id=1, source_target_pairs={{0,32},{1,97},{2,34},{3,99},{4,36},{5,101},{6,38},{7,103},{8,40},{... | collective-permute-start | bytes 786440 | tf_op jit(solution)/shard_map/ppermute | solution.py:396
  114.9 4.8 %collective-permute-start.8 = (f32[80,256]{1,0:T(8,128)S(1)}, f32[80,256]{1,0:T(8,128)S(1)}, u32[]{:S(2)}, u32[]{:S(2)}) collective-permute-start(f32[80,256]{1,0:T(8,128)S(1)} %convert_reduce_fusion), channel_id=1, source_target_pairs={{0,96},{32,0},{64,32},{96,64},{1,97},{33,1},{65,33},{97,65},{2,98}... | collective-permute-start | bytes 245768 | tf_op jit(solution)/shard_map/ppermute | solution.py:387
  114.9 5.9 %collective-permute-start.7 = (f32[80,256]{1,0:T(8,128)S(1)}, f32[80,256]{1,0:T(8,128)S(1)}, u32[]{:S(2)}, u32[]{:S(2)}) collective-permute-start(f32[80,256]{1,0:T(8,128)S(1)} %convert_reduce_fusion), channel_id=1, source_target_pairs={{0,32},{32,64},{64,96},{96,0},{1,33},{33,65},{65,97},{97,1},{2,34}... | collective-permute-start | bytes 245768 | tf_op jit(solution)/shard_map/ppermute | solution.py:387
  117.0 5.9 %collective-permute-start.6 = (f32[80,256]{1,0:T(8,128)S(1)}, f32[80,256]{1,0:T(8,128)S(1)}, u32[]{:S(2)}, u32[]{:S(2)}) collective-permute-start(f32[80,256]{1,0:T(8,128)S(1)} %convert_reduce_fusion), channel_id=1, source_target_pairs={{0,64},{32,96},{64,0},{96,32},{1,65},{33,97},{65,1},{97,33},{2,66}... | collective-permute-start | bytes 245768 | tf_op jit(solution)/shard_map/ppermute | solution.py:387

commit v2 on v1

--- a/solution.py
+++ b/solution.py
@@ -16,7 +16,9 @@
 WIDE = 256
 CHUNK = 4
 PER = MAXB // CHUNK
-UNROLL = 8
+UNROLL = 16
+LOW = 512
+GROUP = 32
 LIST = TB * PER + UNROLL
 MIB = 1024 * 1024
 
@@ -33,9 +35,9 @@
     return lax.dot_general(left, right, NT, preferred_element_type=F32)
 
 
-def one_hot_rows(low_row):
+def one_hot_rows(low_row, count=WIDE):
     n = low_row.shape[1]
-    rows = lax.broadcasted_iota(jnp.int32, (WIDE, n), 0)
+    rows = lax.broadcasted_iota(jnp.int32, (count, n), 0)
     return jnp.where(rows == low_row, 1.0, 0.0).astype(BF16)
 
 
@@ -45,7 +47,7 @@
         return pltpu.make_async_copy(tiles_ref.at[span], buf_ref.at[span], sem_ref.at[chunk])
 
     def block(b, total):
-        chunks = (cnt_ref[0, b] + (CHUNK - 1)) // CHUNK
+        chunks = (cnt_ref[0, b] + (CHUNK - 1)) >> 2
         for k in range(PER):
             list_ref[total + k] = b * PER + k
 
@@ -59,20 +61,21 @@
     for u in range(UNROLL):
         list_ref[total + u] = 0
 
-    def wait():
+    def wait(step):
         def body(i, carry):
             fetch(list_ref[i]).wait()
             return carry
 
-        lax.fori_loop(0, total, body, 0)
+        first = step * UNROLL
+        lax.fori_loop(first, jnp.minimum(first + UNROLL, total), body, 0)
 
     return total, wait
 
 
 def chunk_slots(bid_ref, cnt_ref, list_ref, item, total):
     chunk = list_ref[item]
-    block = chunk // PER
-    first = (chunk % PER) * CHUNK
+    block = chunk >> 2
+    first = (chunk & (PER - 1)) * CHUNK
     count = jnp.where(item < total, cnt_ref[0, block], 0)
     slots = [(bid_ref[0, block, first + j], first + j < count) for j in range(CHUNK)]
     return chunk, block, slots
@@ -111,18 +114,19 @@
     for q in range(TGT // WIDE):
         tgtq_ref[:, q * WIDE:(q + 1) * WIDE] = moved[q * 16:q * 16 + 8]
 
-    group = 32
+    group = GROUP
 
     def gather(i, carry):
         span = pl.ds(pl.multiple_of(i * WIDE, WIDE), WIDE)
         ids = tgtq_ref[:, span]
-        high = jnp.broadcast_to(ids[0:1], (8, WIDE))
-        marks = one_hot_rows(ids[1:2].astype(jnp.int32))
+        whole = (ids[0:1] * float(WIDE) + ids[1:2]).astype(jnp.int32)
+        high = jnp.broadcast_to((whole // LOW).astype(F32), (8, WIDE))
+        marks = one_hot_rows(whole % LOW, LOW)
         acc = [jnp.zeros((8, WIDE), F32) for _ in range(COLS // 8)]
-        for g in range(NODES // WIDE // group):
+        for g in range(NODES // LOW // group):
             left = jnp.concatenate(
                 [
-                    feat_ref[:, (g * group + n) * WIDE:(g * group + n + 1) * WIDE]
+                    feat_ref[:, (g * group + n) * LOW:(g * group + n + 1) * LOW]
                     for n in range(group)
                 ],
                 axis=0,
@@ -138,12 +142,12 @@
         out_ref[2 * i + 1, :COLS] = own[:, BLK:]
         return carry
 
-    lax.fori_loop(0, TGT // WIDE, gather, 0)
+    lax.fori_loop(0, TGT // WIDE, gather, 0, unroll=2)
 
     agg_ref[...] = jnp.zeros_like(agg_ref)
-    wait()
 
     def aggregate(i, carry):
+        wait(i)
         done = []
         for u in range(UNROLL):
             chunk, block, slots = chunk_slots(bid_ref, cnt_ref, list_ref, i * UNROLL + u, total)
@@ -158,7 +162,7 @@
             agg_ref[:, span] += prod
         return carry
 
-    lax.fori_loop(0, (total + UNROLL - 1) // UNROLL, aggregate, 0)
+    lax.fori_loop(0, (total + UNROLL - 1) >> 4, aggregate, 0)
 
     aggregate_rows = agg_ref[...].astype(BF16)
     half = 8
@@ -289,9 +293,9 @@
         rows_ref[:, span] = jnp.concatenate(acc, axis=0).astype(BF16)
 
     grad_ref[...] = jnp.zeros_like(grad_ref)
-    wait()
 
     def spread(i, carry):
+        wait(i)
         done = []
         for u in range(UNROLL):
             chunk, block, slots = chunk_slots(bid_ref, cnt_ref, list_ref, i * UNROLL + u, total)
@@ -305,7 +309,7 @@
                 grad_ref[:, span] += jnp.where(live, piece, 0.0)
         return carry
 
-    lax.fori_loop(0, (total + UNROLL - 1) // UNROLL, spread, 0)
+    lax.fori_loop(0, (total + UNROLL - 1) >> 4, spread, 0)
 
 
 def spread_part(block_ids, counts, back, slots, tiles):
@@ -335,7 +339,7 @@
     per = QUARTER // WIDE
     half = 8
     for step, out_ref in zip(steps, out_refs):
-        which = lax.rem(zid_ref[0] + step, 4)
+        which = (zid_ref[0] + step) & 3
         for g in range(per // half):
             rows = []
             for n in range(half):
@@ -364,23 +368,37 @@
     )(zid, grad, back, tgtq)
 
 
-def place_kernel(zid_ref, a_ref, b_ref, c_ref, d_ref, out_ref):
-    quarter = NODES // 4
-    for step, ref in enumerate((a_ref, b_ref, c_ref, d_ref)):
-        at = pl.multiple_of(lax.rem(zid_ref[0] + step, 4) * quarter, quarter)
-        out_ref[:, pl.ds(at, quarter)] = ref[...].astype(F32)
-
-
-def place(zid, quarters):
+def place_kernel(zid_ref, *refs, steps, fresh):
+    parts = refs[:len(steps)]
+    out_ref, wide_ref, sem = refs[len(steps) + (0 if fresh else 1):]
+    copies = []
+    for k, (step, ref) in enumerate(zip(steps, parts)):
+        at = pl.multiple_of(((zid_ref[0] + step) & 3) * QUARTER, QUARTER)
+        wide_ref[k] = ref[...].astype(F32)
+        copies.append(
+            pltpu.make_async_copy(wide_ref.at[k], out_ref.at[:, pl.ds(at, QUARTER)], sem.at[k])
+        )
+        copies[-1].start()
+    for copy in copies:
+        copy.wait()
+
+
+def place(zid, parts, steps, whole=None):
+    count, fresh = len(steps), whole is None
     return pl.pallas_call(
-        place_kernel,
+        lambda *refs: place_kernel(*refs, steps=steps, fresh=fresh),
         out_shape=jax.ShapeDtypeStruct((COLS, NODES), F32),
-        in_specs=[SMEM] + [VMEM] * 4,
-        out_specs=VMEM,
-        compiler_params=params(32),
+        in_specs=[SMEM] + [VMEM] * count + ([] if fresh else [HBM]),
+        out_specs=HBM,
+        scratch_shapes=[
+            pltpu.VMEM((count, COLS, QUARTER), F32),
+            pltpu.SemaphoreType.DMA((count,)),
+        ],
+        input_output_aliases={} if fresh else {1 + count: 0},
+        compiler_params=params(24),
         cost_estimate=cost(1),
         name="place_quarters",
-    )(zid, *quarters)
+    )(zid, *parts, *(() if fresh else (whole,)))
 
 
 def shift(value, by):
@@ -425,29 +443,28 @@
         exchange(sent), weights, hidden_bias.reshape(1, -1), hidden_grad
     )
     back = exchange(back)
+    back, wgrad = lax.optimization_barrier((back, wgrad))
+    wgrad = exchange(wgrad)
     grad = spread_part(block_ids, counts, back, target_slots, tiles)
     (far2,) = scatter_part(zid, grad, back, tgtq, (2,))
     grad, far2 = lax.optimization_barrier((grad, far2))
-    far1, far3 = scatter_part(zid, grad, back, tgtq, (1, 3))
-    grad, far1, far3, wgrad = lax.optimization_barrier((grad, far1, far3, wgrad))
-    (near,) = scatter_part(zid, grad, back, tgtq, (0,))
-
-    relayed = relay(far2)
-    to_next = far1.astype(F32) + jnp.where(side == 0, relayed, 0).astype(F32)
-    to_last = far3.astype(F32) + jnp.where(side == 1, relayed, 0).astype(F32)
-    from_last, from_next = shift(to_next.astype(BF16), 1), shift(to_last.astype(BF16), 3)
-
-    wgrad = exchange(wgrad)
+    hop = relay(far2)
+    far1, far3, near = scatter_part(zid, grad, back, tgtq, (1, 3, 0))
+    from_last, from_next = shift(far1, 1), shift(far3, 3)
+    from_far = relay(hop)
+    near, wgrad = lax.optimization_barrier((near, wgrad))
+
     wsum = jnp.sum(wgrad.astype(F32), axis=0)
     wsum = (wsum + shift(wsum, 2)) + (shift(wsum, 1) + shift(wsum, 3))
     self_grad = wsum[:COLS]
     neigh_grad = wsum[COLS:2 * COLS]
     bias_grad = wsum[2 * COLS] + (wsum[2 * COLS + 1] + wsum[2 * COLS + 2])
 
-    done = (near + from_last.astype(F32) + from_next.astype(F32)).astype(BF16)
-    of_last, of_next = shift(done, 1), shift(done, 3)
-    of_far = relay(jnp.where(side == 0, of_last, of_next))
-    feature_grad = place(zid, (done, of_next, of_far, of_last))
+    done = near + from_last.astype(F32) + from_next.astype(F32) + from_far.astype(F32)
+    done = done.astype(BF16)
+    of_far, of_next, of_last = shift(done, 2), shift(done, 3), shift(done, 1)
+    feature_grad = place(zid, (done,), (0,))
+    feature_grad = place(zid, (of_next, of_far, of_last), (1, 2, 3), feature_grad)
     return (hidden, feature_grad, self_grad, neigh_grad, bias_grad)
 
 

time: 125 us -> 114 us (0.912)
  waiting for transfers between devices: 37.5 us -> 29.3 us
  starting transfers between devices: 24.9 us -> 30.8 us
  Pallas kernels: 36.4 us -> 31.8 us
  blocking collectives: 18.6 us -> 15.6 us
    all_to_all x3, waiting for transfers between devices: 21.8 us -> 16.8 us  [exchange(): return lax.all_to_all(value, 'feat', 0, 0, tiled=True)]
    ppermute x7 -> x8, starting transfers between devices: 8.62 us -> 12.6 us  [shift(): return lax.ppermute(value, 'dp', [(k, (k + by) % 4) for k in range(4)])]
    ppermute x2, waiting for transfers between devices: 5.16 us -> 1.36 us  [relay(): return lax.ppermute(value, ('dp', 'feat'), pairs)]
    all_to_all x1, blocking collectives: 18.6 us -> 15.6 us  [exchange(): return lax.all_to_all(value, 'feat', 0, 0, tiled=True)]
    pallas_call x1, Pallas kernels: 16.8 us -> 13.8 us  [forward(): pl.pallas_call(forward_kernel, out_shape=(BLOCKS, jax.ShapeDtypeStruct((8...]
    ppermute x2, starting transfers between devices: 0.15 us -> 2.17 us  [relay(): return lax.ppermute(value, ('dp', 'feat'), pairs)]
    pallas_call x1, Pallas kernels: 10.7 us -> 8.82 us  [spread_part(): pl.pallas_call(spread_kernel, out_shape=jax.ShapeDtypeStruct((COLS, NODES...]
    ppermute x7 -> x8, waiting for transfers between devices: 10.6 us -> 11.1 us  [shift(): return lax.ppermute(value, 'dp', [(k, (k + by) % 4) for k in range(4)])]
  transfers between devices with their start and end apart: 12 -> 13, of which waited for: 8 -> 6; matrix products, arithmetic and copies ran while one was open for 1% -> 3% of each run, Pallas kernels for 18% -> 25%
where the time goes in v2:
time: 114 us; the launch traced here: 113 us
  Pallas kernels  31.8 us (28%)
  starting transfers between devices  30.8 us (27%)
  waiting for transfers between devices  29.3 us (26%)
  blocking collectives  15.6 us (14%)
  other arithmetic  3.04 us (3%)
  local copies, waits for them, and re-layouts  1.83 us (2%)
    all_to_all x3, waiting for transfers between devices, exchange(): return lax.all_to_all(value, 'feat', 0, 0, tiled=True)  16.8 us
    all_to_all x3, starting transfers between devices, exchange(): return lax.all_to_all(value, 'feat', 0, 0, tiled=True)  16 us
    all_to_all x1, blocking collectives, exchange(): return lax.all_to_all(value, 'feat', 0, 0, tiled=True)  15.6 us
    pallas_call x1, Pallas kernels, forward(): pl.pallas_call(forward_kernel, out_shape=(BLOCKS, jax.ShapeDtypeStruct((8...  13.8 us
    ppermute x8, starting transfers between devices, shift(): return lax.ppermute(value, 'dp', [(k, (k + by) % 4) for k in range(4)])  12.6 us
    ppermute x8, waiting for transfers between devices, shift(): return lax.ppermute(value, 'dp', [(k, (k + by) % 4) for k in range(4)])  11.1 us
    pallas_call x1, Pallas kernels, spread_part(): pl.pallas_call(spread_kernel, out_shape=jax.ShapeDtypeStruct((COLS, NODES...  8.82 us
    pallas_call x2, Pallas kernels, scatter_part(): pl.pallas_call(lambda *refs: scatter_kernel(*refs, steps=steps), out_shap...  4.75 us
  transfers between devices with their start and end apart: 13, of which 6 were waited for; matrix products, arithmetic and copies ran while one was open for 3% of the time, Pallas kernels for 25%

profile of v2, /device:TPU:0, one launch (start us, length us, event | category | flops | bytes accessed | tf_op | source)
XLA Modules:
  0.0 113.2 jit_solution(2292247095869991991)
XLA Ops:
  0.7 0.8 pad_maximum_fusion
  1.5 1.1 broadcast_in_dim.2
  2.6 7.4 %all-to-all-start = ((bf16[32,64,256]{2,1,0:T(8,128)(2,1)}), bf16[32,64,256]{2,1,0:T(8,128)(2,1)S(1)}, u32[]{:S(2)}, u32[]{:S(2)}) async-start(bf16[32,64,256]{2,1,0:T(8,128)(2,1)} %broadcast_in_dim.2), calls=%async_computation | async-start | bytes 2097152 | tf_op jit(solution)/shard_map/all_to_all | solution.py:418
  10.0 0.1 copy.16.bid_ref
  10.1 13.8 %gather_and_aggregate.1 = (bf16[32,64,128]{2,1,0:T(8,128)(2,1)S(1)}, f32[8,4096]{1,0:T(8,128)S(1)}) custom-call(s32[1,32,16]{2,1,0:T(8,128)S(1)} %copy.16.bid_ref, s32[1,32]{1,0:T(1,128)S(1)} %copy-done.5, bf16[32,16384]{1,0:T(8,128)(2,1)S(1)} %copy-done, s32[1,4096]{1,0:T(1,128)S(1)} %copy-done.2, s32[1,4096]{1,0:T(1,128)S(1)} %copy-done.3, ...), custom_call_target="tpu_custom_call" | custom-call | flops 17301504000 | bytes 55050240 | tf_op jit(solution)/shard_map/gather_and_aggregate/pallas_call | solution.py:208
  24.0 3.4 %all-to-all-done.w_ref = bf16[32,64,256]{2,1,0:T(8,128)(2,1)S(1)} async-done(((bf16[32,64,256]{2,1,0:T(8,128)(2,1)}), bf16[32,64,256]{2,1,0:T(8,128)(2,1)S(1)}, u32[]{:S(2)}, u32[]{:S(2)}) %all-to-all-start) | async-done | bytes 1048608 | tf_op jit(solution)/shard_map/all_to_all | solution.py:418
  27.3 15.6 %all_to_all.20.x_ref = bf16[32,64,128]{2,1,0:T(8,128)(2,1)S(1)} all-to-all(bf16[32,64,128]{2,1,0:T(8,128)(2,1)S(1)} %get-tuple-element.22), channel_id=1, replica_groups=mesh['dp'=4,'feat'=32] {'feat'}, dimensions={0} | all-to-all | bytes 1048576 | tf_op jit(solution)/shard_map/all_to_all | solution.py:418
  42.9 2.4 %hidden_and_slope.1 = (bf16[1,128,256]{2,1,0:T(8,128)(2,1)}, bf16[32,64,128]{2,1,0:T(8,128)(2,1)}, bf16[32,80,256]{2,1,0:T(8,128)(2,1)}) custom-call(bf16[32,64,128]{2,1,0:T(8,128)(2,1)S(1)} %all_to_all.20.x_ref, bf16[32,64,256]{2,1,0:T(8,128)(2,1)S(1)} %all-to-all-done.w_ref, f32[1,256]{1,0:T(1,128)S(1)} %bitcast.4, bf16[1,128,256]{2,1,0:T(8,128)(2,1)S(1)} %copy-done.1), custom_call_target="tpu_custom_call" | custom-call | flops 2306867200 | bytes 7340032 | tf_op jit(solution)/shard_map/hidden_and_slope/pallas_call | solution.py:256
  45.3 3.9 %all-to-all-start.2 = ((bf16[32,64,128]{2,1,0:T(8,128)(2,1)}), bf16[32,64,128]{2,1,0:T(8,128)(2,1)S(1)}, u32[]{:S(2)}, u32[]{:S(2)}) async-start(bf16[32,64,128]{2,1,0:T(8,128)(2,1)} %get-tuple-element.25), calls=%async_computation.2 | async-start | bytes 1048576 | tf_op jit(solution)/shard_map/all_to_all | solution.py:418
  49.2 11.8 %all-to-all-done.2.back_ref.refs_2_ = bf16[32,64,128]{2,1,0:T(8,128)(2,1)S(1)} async-done(((bf16[32,64,128]{2,1,0:T(8,128)(2,1)}), bf16[32,64,128]{2,1,0:T(8,128)(2,1)S(1)}, u32[]{:S(2)}, u32[]{:S(2)}) %all-to-all-start.2) | async-done | bytes 524320 | tf_op jit(solution)/shard_map/all_to_all | solution.py:418
  60.9 4.7 %all-to-all-start.3 = ((bf16[32,80,256]{2,1,0:T(8,128)(2,1)}), bf16[32,80,256]{2,1,0:T(8,128)(2,1)}, u32[]{:S(2)}, u32[]{:S(2)}) async-start(bf16[32,80,256]{2,1,0:T(8,128)(2,1)} %get-tuple-element.31), calls=%async_computation.3 | async-start | bytes 2621440 | tf_op jit(solution)/shard_map/all_to_all | solution.py:418
  65.6 8.8 %spread.1.refs_1_ = f32[32,16384]{1,0:T(8,128)S(1)} custom-call(s32[1,32,16]{2,1,0:T(8,128)S(1)} %copy.16.bid_ref, s32[1,32]{1,0:T(1,128)S(1)} %copy-done.5, bf16[32,64,128]{2,1,0:T(8,128)(2,1)S(1)} %all-to-all-done.2.back_ref.refs_2_, s32[1,4096]{1,0:T(1,128)S(1)} %copy-done.3, bf16[512,128,128]{2,1,0:T(8,128)(2,1)} %bitcast.7), custom_call_target="tpu_custom_call" | custom-call | flops 8074035200 | bytes 25690112 | tf_op jit(solution)/shard_map/spread/pallas_call | solution.py:316
  74.5 1.3 %scatter.2 = bf16[32,4096]{1,0:T(8,128)(2,1)S(1)} custom-call(s32[1]{0:T(128)} %bitcast.2.refs_0_, f32[32,16384]{1,0:T(8,128)S(1)} %spread.1.refs_1_, bf16[32,64,128]{2,1,0:T(8,128)(2,1)S(1)} %all-to-all-done.2.back_ref.refs_2_, f32[8,4096]{1,0:T(8,128)S(1)} %get-tuple-element.28.refs_3_), custom_call_target="tpu_custom_call" | custom-call | flops 2306867200 | bytes 7340032 | tf_op jit(solution)/shard_map/scatter/pallas_call | solution.py:357
  75.7 2.2 %collective-permute-start.2 = (bf16[32,4096]{1,0:T(8,128)(2,1)S(1)}, bf16[32,4096]{1,0:T(8,128)(2,1)S(1)}, u32[]{:S(2)}, u32[]{:S(2)}) collective-permute-start(bf16[32,4096]{1,0:T(8,128)(2,1)S(1)} %scatter.2), channel_id=1, source_target_pairs={{0,32},{1,97},{2,34},{3,99},{4,36},{5,101},{6,38},{7,103},{8,40},{... | collective-permute-start | bytes 786440 | tf_op jit(solution)/shard_map/ppermute | solution.py:414
  77.9 3.5 %scatter.3 = (bf16[32,4096]{1,0:T(8,128)(2,1)S(1)}, bf16[32,4096]{1,0:T(8,128)(2,1)S(1)}, f32[32,4096]{1,0:T(8,128)S(1)}) custom-call(s32[1]{0:T(128)} %bitcast.2.refs_0_, f32[32,16384]{1,0:T(8,128)S(1)} %spread.1.refs_1_, bf16[32,64,128]{2,1,0:T(8,128)(2,1)S(1)} %all-to-all-done.2.back_ref.refs_2_, f32[8,4096]{1,0:T(8,128)S(1)} %get-tuple-element.28.refs_3_), custom_call_target="tpu_custom_call" | custom-call | flops 4613734400 | bytes 14680064 | tf_op jit(solution)/shard_map/scatter/pallas_call | solution.py:357
  81.4 0.6 collective-permute-start
  82.0 2.7 %collective-permute-start.1 = (bf16[32,4096]{1,0:T(8,128)(2,1)S(1)}, bf16[32,4096]{1,0:T(8,128)(2,1)S(1)}, u32[]{:S(2)}, u32[]{:S(2)}) collective-permute-start(bf16[32,4096]{1,0:T(8,128)(2,1)S(1)} %get-tuple-element.34), channel_id=1, source_target_pairs={{0,96},{32,0},{64,32},{96,64},{1,97},{33,1},{65,33},{97,65},{2,98}... | collective-permute-start | bytes 786440 | tf_op jit(solution)/shard_map/ppermute | solution.py:405
  84.7 1.7 %all-to-all-done.3 = bf16[32,80,256]{2,1,0:T(8,128)(2,1)} async-done(((bf16[32,80,256]{2,1,0:T(8,128)(2,1)}), bf16[32,80,256]{2,1,0:T(8,128)(2,1)}, u32[]{:S(2)}, u32[]{:S(2)}) %all-to-all-start.3) | async-done | bytes 1310752 | tf_op jit(solution)/shard_map/all_to_all | solution.py:418
  86.4 1.5 %convert_reduce_fusion = f32[80,256]{1,0:T(8,128)S(1)} fusion(bf16[32,80,256]{2,1,0:T(8,128)(2,1)} %all-to-all-done.3), kind=kLoop, calls=%fused_computation | loop fusion | flops 1290240 | bytes 1392640 | tf_op jit(solution)/shard_map/reduce_sum | solution.py:457
  87.9 3.7 %collective-permute-start.9 = (f32[80,256]{1,0:T(8,128)S(1)}, f32[80,256]{1,0:T(8,128)S(1)}, u32[]{:S(2)}, u32[]{:S(2)}) collective-permute-start(f32[80,256]{1,0:T(8,128)S(1)} %convert_reduce_fusion), channel_id=1, source_target_pairs={{0,96},{32,0},{64,32},{96,64},{1,97},{33,1},{65,33},{97,65},{2,98}... | collective-permute-start | bytes 245768 | tf_op jit(solution)/shard_map/ppermute | solution.py:405
  91.6 1.9 %collective-permute-start.7 = (f32[80,256]{1,0:T(8,128)S(1)}, f32[80,256]{1,0:T(8,128)S(1)}, u32[]{:S(2)}, u32[]{:S(2)}) collective-permute-start(f32[80,256]{1,0:T(8,128)S(1)} %convert_reduce_fusion), channel_id=1, source_target_pairs={{0,64},{32,96},{64,0},{96,32},{1,65},{33,97},{65,1},{97,33},{2,66}... | collective-permute-start | bytes 245768 | tf_op jit(solution)/shard_map/ppermute | solution.py:405
  93.5 1.4 %collective-permute-done.3 = bf16[32,4096]{1,0:T(8,128)(2,1)S(1)} collective-permute-done((bf16[32,4096]{1,0:T(8,128)(2,1)S(1)}, bf16[32,4096]{1,0:T(8,128)(2,1)S(1)}, u32[]{:S(2)}, u32[]{:S(2)}) %collective-permute-start.3) | collective-permute-done | bytes 262176 | tf_op jit(solution)/shard_map/ppermute | solution.py:414
  94.8 0.1 add_convert_fusion.refs_1_
  94.9 0.9 collective-permute-start.6
  95.9 0.8 collective-permute-start.5
  96.7 0.8 place_quarters.2.refs_4_
  97.5 2.0 %collective-permute-start.4 = (bf16[32,4096]{1,0:T(8,128)(2,1)S(1)}, bf16[32,4096]{1,0:T(8,128)(2,1)S(1)}, u32[]{:S(2)}, u32[]{:S(2)}) collective-permute-start(bf16[32,4096]{1,0:T(8,128)(2,1)S(1)} %add_convert_fusion.refs_1_), channel_id=1, source_target_pairs={{0,96},{32,0},{64,32},{96,64},{1,97},{33,1},{65,33},{97,65},{2,98}... | collective-permute-start | bytes 786440 | tf_op jit(solution)/shard_map/ppermute | solution.py:405
  99.6 0.6 fusion
  100.2 0.6 fusion.1
  100.8 9.9 %collective-permute-done.6.refs_3_ = bf16[32,4096]{1,0:T(8,128)(2,1)S(1)} collective-permute-done((bf16[32,4096]{1,0:T(8,128)(2,1)S(1)}, bf16[32,4096]{1,0:T(8,128)(2,1)S(1)}, u32[]{:S(2)}, u32[]{:S(2)}) %collective-permute-start.6) | collective-permute-done | bytes 262176 | tf_op jit(solution)/shard_map/ppermute | solution.py:405
  110.7 1.1 collective-permute-done.4.refs_1_
  111.8 1.2 %place_quarters.3 = f32[32,16384]{1,0:T(8,128)} custom-call(s32[1]{0:T(128)} %bitcast.2.refs_0_, bf16[32,4096]{1,0:T(8,128)(2,1)S(1)} %collective-permute-done.4.refs_1_, bf16[32,4096]{1,0:T(8,128)(2,1)S(1)} %collective-permute-done.5.refs_2_, bf16[32,4096]{1,0:T(8,128)(2,1)S(1)} %collective-permute-done.6.refs_3_, ...), custom_call_target="tpu_custom_call", output_to_operand_aliasing={{}: (4, {})} | custom-call | flops 1153433600 | bytes 3670016 | tf_op jit(solution)/shard_map/place_quarters/pallas_call | solution.py:388
  (24 shorter events, 0.1 us)
Async XLA Ops:
  0.6 9.4 %copy-start.6 = (s32[1,32,16]{1,2,0:T(8,128)S(1)}, s32[1,32,16]{1,2,0:T(8,128)}, u32[]{:S(2)}) copy-start(s32[1,32,16]{1,2,0:T(8,128)} %param.12) | copy-start | bytes 6148
  0.6 9.5 %copy-start.3 = (s32[1,4096]{1,0:T(1,128)S(1)}, s32[1,4096]{1,0:T(1,128)}, u32[]{:S(2)}) copy-start(s32[1,4096]{1,0:T(1,128)} %slot_ref.3) | copy-start | bytes 49156
  0.7 9.4 %copy-start.5 = (s32[1,32]{1,0:T(1,128)S(1)}, s32[1,32]{1,0:T(1,128)}, u32[]{:S(2)}) copy-start(s32[1,32]{1,0:T(1,128)} %cnt_ref.3) | copy-start | bytes 388
  0.7 9.4 %copy-start.2 = (s32[1,4096]{1,0:T(1,128)S(1)}, s32[1,4096]{1,0:T(1,128)}, u32[]{:S(2)}) copy-start(s32[1,4096]{1,0:T(1,128)} %tgt_ref.1) | copy-start | bytes 49156
  0.7 9.4 %copy-start = (bf16[32,16384]{1,0:T(8,128)(2,1)S(1)}, bf16[32,16384]{1,0:T(8,128)(2,1)}, u32[]{:S(2)}) copy-start(bf16[32,16384]{1,0:T(8,128)(2,1)} %feat_ref.1) | copy-start | bytes 3145732
  2.6 24.7 %all-to-all-start = ((bf16[32,64,256]{2,1,0:T(8,128)(2,1)}), bf16[32,64,256]{2,1,0:T(8,128)(2,1)S(1)}, u32[]{:S(2)}, u32[]{:S(2)}) async-start(bf16[32,64,256]{2,1,0:T(8,128)(2,1)} %broadcast_in_dim.2), calls=%async_computation | async-start | bytes 2097152 | tf_op jit(solution)/shard_map/all_to_all | solution.py:418
  10.1 32.8 %copy-start.1 = (bf16[1,128,256]{2,1,0:T(8,128)(2,1)S(1)}, bf16[1,128,256]{2,1,0:T(8,128)(2,1)}, u32[]{:S(2)}) copy-start(bf16[1,128,256]{2,1,0:T(8,128)(2,1)} %grad_ref.1) | copy-start | bytes 196612
  10.1 32.8 %copy-start.4 = (f32[256]{0:T(256)S(1)}, f32[256]{0:T(256)}, u32[]{:S(2)}) copy-start(f32[256]{0:T(256)} %param.18) | copy-start | bytes 3076
  45.3 15.7 %all-to-all-start.2 = ((bf16[32,64,128]{2,1,0:T(8,128)(2,1)}), bf16[32,64,128]{2,1,0:T(8,128)(2,1)S(1)}, u32[]{:S(2)}, u32[]{:S(2)}) async-start(bf16[32,64,128]{2,1,0:T(8,128)(2,1)} %get-tuple-element.25), calls=%async_computation.2 | async-start | bytes 1048576 | tf_op jit(solution)/shard_map/all_to_all | solution.py:418
  60.9 25.5 %all-to-all-start.3 = ((bf16[32,80,256]{2,1,0:T(8,128)(2,1)}), bf16[32,80,256]{2,1,0:T(8,128)(2,1)}, u32[]{:S(2)}, u32[]{:S(2)}) async-start(bf16[32,80,256]{2,1,0:T(8,128)(2,1)} %get-tuple-element.31), calls=%async_computation.3 | async-start | bytes 2621440 | tf_op jit(solution)/shard_map/all_to_all | solution.py:418
  75.7 9.0 %collective-permute-start.2 = (bf16[32,4096]{1,0:T(8,128)(2,1)S(1)}, bf16[32,4096]{1,0:T(8,128)(2,1)S(1)}, u32[]{:S(2)}, u32[]{:S(2)}) collective-permute-start(bf16[32,4096]{1,0:T(8,128)(2,1)S(1)} %scatter.2), channel_id=1, source_target_pairs={{0,32},{1,97},{2,34},{3,99},{4,36},{5,101},{6,38},{7,103},{8,40},{... | collective-permute-start | bytes 786440 | tf_op jit(solution)/shard_map/ppermute | solution.py:414
  81.4 10.2 %collective-permute-start = (bf16[32,4096]{1,0:T(8,128)(2,1)S(1)}, bf16[32,4096]{1,0:T(8,128)(2,1)S(1)}, u32[]{:S(2)}, u32[]{:S(2)}) collective-permute-start(bf16[32,4096]{1,0:T(8,128)(2,1)S(1)} %get-tuple-element.33), channel_id=1, source_target_pairs={{0,32},{32,64},{64,96},{96,0},{1,33},{33,65},{65,97},{97,1},{2,34}... | collective-permute-start | bytes 786440 | tf_op jit(solution)/shard_map/ppermute | solution.py:405
  82.0 11.4 %collective-permute-start.1 = (bf16[32,4096]{1,0:T(8,128)(2,1)S(1)}, bf16[32,4096]{1,0:T(8,128)(2,1)S(1)}, u32[]{:S(2)}, u32[]{:S(2)}) collective-permute-start(bf16[32,4096]{1,0:T(8,128)(2,1)S(1)} %get-tuple-element.34), channel_id=1, source_target_pairs={{0,96},{32,0},{64,32},{96,64},{1,97},{33,1},{65,33},{97,65},{2,98}... | collective-permute-start | bytes 786440 | tf_op jit(solution)/shard_map/ppermute | solution.py:405
  84.7 10.1 %collective-permute-start.3 = (bf16[32,4096]{1,0:T(8,128)(2,1)S(1)}, bf16[32,4096]{1,0:T(8,128)(2,1)S(1)}, u32[]{:S(2)}, u32[]{:S(2)}) collective-permute-start(bf16[32,4096]{1,0:T(8,128)(2,1)S(1)} %collective-permute-done.2), channel_id=1, source_target_pairs={{0,32},{1,97},{2,34},{3,99},{4,36},{5,101},{6,38},{7,103},{8,40},{... | collective-permute-start | bytes 786440 | tf_op jit(solution)/shard_map/ppermute | solution.py:414
  87.9 9.6 %collective-permute-start.9 = (f32[80,256]{1,0:T(8,128)S(1)}, f32[80,256]{1,0:T(8,128)S(1)}, u32[]{:S(2)}, u32[]{:S(2)}) collective-permute-start(f32[80,256]{1,0:T(8,128)S(1)} %convert_reduce_fusion), channel_id=1, source_target_pairs={{0,96},{32,0},{64,32},{96,64},{1,97},{33,1},{65,33},{97,65},{2,98}... | collective-permute-start | bytes 245768 | tf_op jit(solution)/shard_map/ppermute | solution.py:405
  91.6 8.0 %collective-permute-start.8 = (f32[80,256]{1,0:T(8,128)S(1)}, f32[80,256]{1,0:T(8,128)S(1)}, u32[]{:S(2)}, u32[]{:S(2)}) collective-permute-start(f32[80,256]{1,0:T(8,128)S(1)} %convert_reduce_fusion), channel_id=1, source_target_pairs={{0,32},{32,64},{64,96},{96,0},{1,33},{33,65},{65,97},{97,1},{2,34}... | collective-permute-start | bytes 245768 | tf_op jit(solution)/shard_map/ppermute | solution.py:405
  91.6 8.0 %collective-permute-start.7 = (f32[80,256]{1,0:T(8,128)S(1)}, f32[80,256]{1,0:T(8,128)S(1)}, u32[]{:S(2)}, u32[]{:S(2)}) collective-permute-start(f32[80,256]{1,0:T(8,128)S(1)} %convert_reduce_fusion), channel_id=1, source_target_pairs={{0,64},{32,96},{64,0},{96,32},{1,65},{33,97},{65,1},{97,33},{2,66}... | collective-permute-start | bytes 245768 | tf_op jit(solution)/shard_map/ppermute | solution.py:405
  94.9 15.8 %collective-permute-start.6 = (bf16[32,4096]{1,0:T(8,128)(2,1)S(1)}, bf16[32,4096]{1,0:T(8,128)(2,1)S(1)}, u32[]{:S(2)}, u32[]{:S(2)}) collective-permute-start(bf16[32,4096]{1,0:T(8,128)(2,1)S(1)} %add_convert_fusion.refs_1_), channel_id=1, source_target_pairs={{0,32},{32,64},{64,96},{96,0},{1,33},{33,65},{65,97},{97,1},{2,34}... | collective-permute-start | bytes 786440 | tf_op jit(solution)/shard_map/ppermute | solution.py:405
  95.9 14.9 %collective-permute-start.5 = (bf16[32,4096]{1,0:T(8,128)(2,1)S(1)}, bf16[32,4096]{1,0:T(8,128)(2,1)S(1)}, u32[]{:S(2)}, u32[]{:S(2)}) collective-permute-start(bf16[32,4096]{1,0:T(8,128)(2,1)S(1)} %add_convert_fusion.refs_1_), channel_id=1, source_target_pairs={{0,64},{32,96},{64,0},{96,32},{1,65},{33,97},{65,1},{97,33},{2,66}... | collective-permute-start | bytes 786440 | tf_op jit(solution)/shard_map/ppermute | solution.py:405
  97.5 14.3 %collective-permute-start.4 = (bf16[32,4096]{1,0:T(8,128)(2,1)S(1)}, bf16[32,4096]{1,0:T(8,128)(2,1)S(1)}, u32[]{:S(2)}, u32[]{:S(2)}) collective-permute-start(bf16[32,4096]{1,0:T(8,128)(2,1)S(1)} %add_convert_fusion.refs_1_), channel_id=1, source_target_pairs={{0,96},{32,0},{64,32},{96,64},{1,97},{33,1},{65,33},{97,65},{2,98}... | collective-permute-start | bytes 786440 | tf_op jit(solution)/shard_map/ppermute | solution.py:405

commit v3 on v2

--- a/solution.py
+++ b/solution.py
@@ -222,7 +222,7 @@
 
 
 def middle_kernel(
-    x_ref, w_ref, bias_ref, grad_ref, hidden_ref, back_ref, wgrad_ref
+    x_ref, w_ref, bias_ref, grad_ref, hidden_ref, back_ref, slope_ref
 ):
     half = FEAT * COLS
     x_own = x_ref[:, :COLS].reshape(half, BLK)
@@ -238,6 +238,14 @@
     slope = (grad_ref[0].astype(F32) * sig * (1.0 + preact * (1.0 - sig))).astype(BF16)
     back_ref[:, :COLS] = dot_nt(w_own, slope).astype(BF16).reshape(FEAT, COLS, BLK)
     back_ref[:, COLS:] = dot_nt(w_agg, slope).astype(BF16).reshape(FEAT, COLS, BLK)
+    slope_ref[...] = slope
+
+
+def weight_kernel(x_ref, slope_ref, wgrad_ref):
+    half = FEAT * COLS
+    slope = slope_ref[...]
+    x_own = x_ref[:, :COLS].reshape(half, BLK)
+    x_agg = x_ref[:, COLS:].reshape(half, BLK)
     wgrad_ref[:, :COLS] = dot(x_own, slope).astype(BF16).reshape(FEAT, COLS, WIDE)
     wgrad_ref[:, COLS:2 * COLS] = dot(x_agg, slope).astype(BF16).reshape(FEAT, COLS, WIDE)
     total = jnp.sum(slope.astype(F32), axis=0, keepdims=True)
@@ -252,13 +260,25 @@
     wgrad_ref[:, 2 * COLS:] = jnp.broadcast_to(tail[None], (FEAT, 16, WIDE))
 
 
+def weight_part(x, slope):
+    return pl.pallas_call(
+        weight_kernel,
+        out_shape=jax.ShapeDtypeStruct((FEAT, 2 * COLS + 16, WIDE), BF16),
+        in_specs=[VMEM] * 2,
+        out_specs=VMEM,
+        compiler_params=params(24),
+        cost_estimate=cost(2),
+        name="weight_partials",
+    )(x, slope)
+
+
 def middle(x, w, bias, grad):
     return pl.pallas_call(
         middle_kernel,
         out_shape=(
             jax.ShapeDtypeStruct((1, BLK, WIDE), BF16),
             BLOCKS,
-            jax.ShapeDtypeStruct((FEAT, 2 * COLS + 16, WIDE), BF16),
+            jax.ShapeDtypeStruct((BLK, WIDE), BF16),
         ),
         in_specs=[VMEM] * 4,
         out_specs=(VMEM,) * 3,
@@ -328,8 +348,8 @@
 QUARTER = NODES // 4
 
 
-def scatter_kernel(zid_ref, grad_ref, back_ref, tgtq_ref, *refs, steps):
-    out_refs, mark_ref = refs[:-1], refs[-1]
+def scatter_kernel(zid_ref, grad_ref, back_ref, tgtq_ref, *refs, steps, plus):
+    extra_refs, out_refs, mark_ref = refs[:plus], refs[plus:-1], refs[-1]
     ids = tgtq_ref[...]
     for i in range(TGT // WIDE):
         span = slice(i * WIDE, (i + 1) * WIDE)
@@ -350,22 +370,24 @@
                 at = (g * half + n) * WIDE
                 span = pl.ds(pl.multiple_of(which * QUARTER + at, WIDE), WIDE)
                 value = grad_ref[:, span] + prod[n * COLS:(n + 1) * COLS]
+                for ref in extra_refs:
+                    value = value + ref[:, at:at + WIDE].astype(F32)
                 out_ref[:, at:at + WIDE] = value.astype(out_ref.dtype)
 
 
-def scatter_part(zid, grad, back, tgtq, steps):
+def scatter_part(zid, grad, back, tgtq, steps, *extra):
     return pl.pallas_call(
-        lambda *refs: scatter_kernel(*refs, steps=steps),
+        lambda *refs: scatter_kernel(*refs, steps=steps, plus=len(extra)),
         out_shape=tuple(
             jax.ShapeDtypeStruct((COLS, QUARTER), BF16 if step else F32) for step in steps
         ),
-        in_specs=[SMEM, VMEM, VMEM, VMEM],
+        in_specs=[SMEM] + [VMEM] * (3 + len(extra)),
         out_specs=tuple(VMEM for _ in steps),
         scratch_shapes=[pltpu.VMEM((WIDE, TGT), BF16)],
         compiler_params=params(24),
-        cost_estimate=cost(1 + len(steps)),
+        cost_estimate=cost(15 if extra else 1 + len(steps)),
         name="scatter",
-    )(zid, grad, back, tgtq)
+    )(zid, grad, back, tgtq, *extra)
 
 
 def place_kernel(zid_ref, *refs, steps, fresh):
@@ -405,15 +427,6 @@
     return lax.ppermute(value, "dp", [(k, (k + by) % 4) for k in range(4)])
 
 
-def relay(value):
-    pairs = [
-        (k * FEAT + f, ((k + (1 if f % 2 == 0 else 3)) % 4) * FEAT + f)
-        for k in range(4)
-        for f in range(FEAT)
-    ]
-    return lax.ppermute(value, ("dp", "feat"), pairs)
-
-
 def exchange(value):
     return lax.all_to_all(value, "feat", 0, 0, tiled=True)
 
@@ -439,32 +452,32 @@
     weights = exchange(jnp.broadcast_to(weights[None], (FEAT, 2 * COLS, WIDE)))
     sent, tgtq = forward(block_ids, counts, features, targets, target_slots, tiles)
     sent, weights = lax.optimization_barrier((sent, weights))
-    hidden, back, wgrad = middle(
-        exchange(sent), weights, hidden_bias.reshape(1, -1), hidden_grad
-    )
+    got = exchange(sent)
+    hidden, back, slope = middle(got, weights, hidden_bias.reshape(1, -1), hidden_grad)
     back = exchange(back)
+    wgrad = weight_part(got, slope)
     back, wgrad = lax.optimization_barrier((back, wgrad))
     wgrad = exchange(wgrad)
     grad = spread_part(block_ids, counts, back, target_slots, tiles)
     (far2,) = scatter_part(zid, grad, back, tgtq, (2,))
     grad, far2 = lax.optimization_barrier((grad, far2))
-    hop = relay(far2)
-    far1, far3, near = scatter_part(zid, grad, back, tgtq, (1, 3, 0))
+    from_far = shift(far2, 2)
+    far1, far3 = scatter_part(zid, grad, back, tgtq, (1, 3))
     from_last, from_next = shift(far1, 1), shift(far3, 3)
-    from_far = relay(hop)
+    (near,) = scatter_part(zid, grad, back, tgtq, (0,), from_far)
     near, wgrad = lax.optimization_barrier((near, wgrad))
 
-    wsum = jnp.sum(wgrad.astype(F32), axis=0)
+    wsum = jnp.sum(wgrad[:, :2 * COLS + 8].astype(F32), axis=0)
     wsum = (wsum + shift(wsum, 2)) + (shift(wsum, 1) + shift(wsum, 3))
     self_grad = wsum[:COLS]
     neigh_grad = wsum[COLS:2 * COLS]
     bias_grad = wsum[2 * COLS] + (wsum[2 * COLS + 1] + wsum[2 * COLS + 2])
 
-    done = near + from_last.astype(F32) + from_next.astype(F32) + from_far.astype(F32)
+    done = near + from_last.astype(F32) + from_next.astype(F32)
     done = done.astype(BF16)
     of_far, of_next, of_last = shift(done, 2), shift(done, 3), shift(done, 1)
-    feature_grad = place(zid, (done,), (0,))
-    feature_grad = place(zid, (of_next, of_far, of_last), (1, 2, 3), feature_grad)
+    feature_grad = place(zid, (done, of_far), (0, 2))
+    feature_grad = place(zid, (of_next, of_last), (1, 3), feature_grad)
     return (hidden, feature_grad, self_grad, neigh_grad, bias_grad)
 
 

time: 114 us -> 112 us (0.982)
  waiting for transfers between devices: 29.3 us -> 22 us
  starting transfers between devices: 30.8 us -> 36.9 us
    ppermute x8 -> x9, starting transfers between devices: 12.6 us -> 20.9 us  [shift(): return lax.ppermute(value, 'dp', [(k, (k + by) % 4) for k in range(4)])]
    ppermute x8 -> x9, waiting for transfers between devices: 11.1 us -> 7.66 us  [shift(): return lax.ppermute(value, 'dp', [(k, (k + by) % 4) for k in range(4)])]
    all_to_all x3, waiting for transfers between devices: 16.8 us -> 14.4 us  [exchange(): return lax.all_to_all(value, 'feat', 0, 0, tiled=True)]
    ppermute x2 -> x0, starting transfers between devices: 2.17 us -> none  [relay(): return lax.ppermute(value, ('dp', 'feat'), pairs)]
    pallas_call x2 -> x4, Pallas kernels: 4.75 us -> 6.43 us  [the longest x3 4.96 us: scatter_part(): pl.pallas_call(lambda *refs: scatter_kernel(*refs, steps=steps, plus=len(...]
    ppermute x2 -> x0, waiting for transfers between devices: 1.36 us -> none  [relay(): return lax.ppermute(value, ('dp', 'feat'), pairs)]
  transfers between devices with their start and end apart: 13 -> 12, of which waited for: 6 -> 7; matrix products, arithmetic and copies ran while one was open for 3% -> 3% of each run, Pallas kernels for 25% -> 26%
where the time goes in v3:
time: 112 us; the launch traced here: 111 us
  starting transfers between devices  36.9 us (33%)
  Pallas kernels  31.2 us (28%)
  waiting for transfers between devices  22 us (20%)
  blocking collectives  15.1 us (13%)
  other arithmetic  2.95 us (3%)
  local copies, waits for them, and re-layouts  1.83 us (2%)
    ppermute x9, starting transfers between devices, shift(): return lax.ppermute(value, 'dp', [(k, (k + by) % 4) for k in range(4)])  20.9 us
    all_to_all x3, starting transfers between devices, exchange(): return lax.all_to_all(value, 'feat', 0, 0, tiled=True)  16 us
    all_to_all x1, blocking collectives, exchange(): return lax.all_to_all(value, 'feat', 0, 0, tiled=True)  15.1 us
    all_to_all x3, waiting for transfers between devices, exchange(): return lax.all_to_all(value, 'feat', 0, 0, tiled=True)  14.4 us
    pallas_call x1, Pallas kernels, forward(): pl.pallas_call(forward_kernel, out_shape=(BLOCKS, jax.ShapeDtypeStruct((8...  13.1 us
    pallas_call x1, Pallas kernels, spread_part(): pl.pallas_call(spread_kernel, out_shape=jax.ShapeDtypeStruct((COLS, NODES...  7.81 us
    ppermute x9, waiting for transfers between devices, shift(): return lax.ppermute(value, 'dp', [(k, (k + by) % 4) for k in range(4)])  7.66 us
    pallas_call x3, Pallas kernels, scatter_part(): pl.pallas_call(lambda *refs: scatter_kernel(*refs, steps=steps, plus=len(...  4.96 us
  transfers between devices with their start and end apart: 12, of which 7 were waited for; matrix products, arithmetic and copies ran while one was open for 3% of the time, Pallas kernels for 26%

profile of v3, /device:TPU:0, one launch (start us, length us, event | category | flops | bytes accessed | tf_op | source)
XLA Modules:
  0.0 111.0 jit_solution(7752204227988054955)
XLA Ops:
  0.7 0.8 pad_maximum_fusion
  1.5 1.1 broadcast_in_dim.2
  2.6 7.4 %all-to-all-start = ((bf16[32,64,256]{2,1,0:T(8,128)(2,1)}), bf16[32,64,256]{2,1,0:T(8,128)(2,1)S(1)}, u32[]{:S(2)}, u32[]{:S(2)}) async-start(bf16[32,64,256]{2,1,0:T(8,128)(2,1)} %broadcast_in_dim.2), calls=%async_computation | async-start | bytes 2097152 | tf_op jit(solution)/shard_map/all_to_all | solution.py:431
  10.1 13.1 %gather_and_aggregate.1 = (bf16[32,64,128]{2,1,0:T(8,128)(2,1)S(1)}, f32[8,4096]{1,0:T(8,128)S(1)}) custom-call(s32[1,32,16]{2,1,0:T(8,128)S(1)} %copy.16.bid_ref, s32[1,32]{1,0:T(1,128)S(1)} %copy-done.5, bf16[32,16384]{1,0:T(8,128)(2,1)S(1)} %copy-done, s32[1,4096]{1,0:T(1,128)S(1)} %copy-done.2, s32[1,4096]{1,0:T(1,128)S(1)} %copy-done.3, ...), custom_call_target="tpu_custom_call" | custom-call | flops 17301504000 | bytes 55050240 | tf_op jit(solution)/shard_map/gather_and_aggregate/pallas_call | solution.py:208
  23.3 4.1 %all-to-all-done.w_ref = bf16[32,64,256]{2,1,0:T(8,128)(2,1)S(1)} async-done(((bf16[32,64,256]{2,1,0:T(8,128)(2,1)}), bf16[32,64,256]{2,1,0:T(8,128)(2,1)S(1)}, u32[]{:S(2)}, u32[]{:S(2)}) %all-to-all-start) | async-done | bytes 1048608 | tf_op jit(solution)/shard_map/all_to_all | solution.py:431
  27.3 15.1 %all_to_all.20.x_ref = bf16[32,64,128]{2,1,0:T(8,128)(2,1)S(1)} all-to-all(bf16[32,64,128]{2,1,0:T(8,128)(2,1)S(1)} %get-tuple-element.21), channel_id=1, replica_groups=mesh['dp'=4,'feat'=32] {'feat'}, dimensions={0} | all-to-all | bytes 1048576 | tf_op jit(solution)/shard_map/all_to_all | solution.py:431
  42.5 1.8 %hidden_and_slope.1 = (bf16[1,128,256]{2,1,0:T(8,128)(2,1)}, bf16[32,64,128]{2,1,0:T(8,128)(2,1)}, bf16[128,256]{1,0:T(8,128)(2,1)S(1)}) custom-call(bf16[32,64,128]{2,1,0:T(8,128)(2,1)S(1)} %all_to_all.20.x_ref, bf16[32,64,256]{2,1,0:T(8,128)(2,1)S(1)} %all-to-all-done.w_ref, f32[1,256]{1,0:T(1,128)S(1)} %bitcast.4, bf16[1,128,256]{2,1,0:T(8,128)(2,1)S(1)} %copy-done.1), custom_call_target="tpu_custom_call" | custom-call | flops 2306867200 | bytes 7340032 | tf_op jit(solution)/shard_map/hidden_and_slope/pallas_call | solution.py:276
  44.3 3.9 %all-to-all-start.2 = ((bf16[32,64,128]{2,1,0:T(8,128)(2,1)}), bf16[32,64,128]{2,1,0:T(8,128)(2,1)S(1)}, u32[]{:S(2)}, u32[]{:S(2)}) async-start(bf16[32,64,128]{2,1,0:T(8,128)(2,1)} %get-tuple-element.24), calls=%async_computation.2 | async-start | bytes 1048576 | tf_op jit(solution)/shard_map/all_to_all | solution.py:431
  48.2 1.5 %weight_partials.1 = bf16[32,80,256]{2,1,0:T(8,128)(2,1)} custom-call(bf16[32,64,128]{2,1,0:T(8,128)(2,1)S(1)} %all_to_all.20.x_ref, bf16[128,256]{1,0:T(8,128)(2,1)S(1)} %get-tuple-element.25.slope_ref), custom_call_target="tpu_custom_call" | custom-call | flops 2306867200 | bytes 7340032 | tf_op jit(solution)/shard_map/weight_partials/pallas_call | solution.py:264
  49.6 10.3 %all-to-all-done.2.back_ref.refs_2_ = bf16[32,64,128]{2,1,0:T(8,128)(2,1)S(1)} async-done(((bf16[32,64,128]{2,1,0:T(8,128)(2,1)}), bf16[32,64,128]{2,1,0:T(8,128)(2,1)S(1)}, u32[]{:S(2)}, u32[]{:S(2)}) %all-to-all-start.2) | async-done | bytes 524320 | tf_op jit(solution)/shard_map/all_to_all | solution.py:431
  59.9 4.7 %all-to-all-start.3 = ((bf16[32,80,256]{2,1,0:T(8,128)(2,1)}), bf16[32,80,256]{2,1,0:T(8,128)(2,1)}, u32[]{:S(2)}, u32[]{:S(2)}) async-start(bf16[32,80,256]{2,1,0:T(8,128)(2,1)} %weight_partials.1), calls=%async_computation.3 | async-start | bytes 2621440 | tf_op jit(solution)/shard_map/all_to_all | solution.py:431
  64.6 7.8 %spread.1.refs_1_ = f32[32,16384]{1,0:T(8,128)S(1)} custom-call(s32[1,32,16]{2,1,0:T(8,128)S(1)} %copy.16.bid_ref, s32[1,32]{1,0:T(1,128)S(1)} %copy-done.5, bf16[32,64,128]{2,1,0:T(8,128)(2,1)S(1)} %all-to-all-done.2.back_ref.refs_2_, s32[1,4096]{1,0:T(1,128)S(1)} %copy-done.3, bf16[512,128,128]{2,1,0:T(8,128)(2,1)} %bitcast.7), custom_call_target="tpu_custom_call" | custom-call | flops 8074035200 | bytes 25690112 | tf_op jit(solution)/shard_map/spread/pallas_call | solution.py:336
  72.4 1.3 %scatter.3 = bf16[32,4096]{1,0:T(8,128)(2,1)S(1)} custom-call(s32[1]{0:T(128)} %bitcast.2.refs_0_, f32[32,16384]{1,0:T(8,128)S(1)} %spread.1.refs_1_, bf16[32,64,128]{2,1,0:T(8,128)(2,1)S(1)} %all-to-all-done.2.back_ref.refs_2_, f32[8,4096]{1,0:T(8,128)S(1)} %get-tuple-element.27.refs_3_), custom_call_target="tpu_custom_call" | custom-call | flops 2306867200 | bytes 7340032 | tf_op jit(solution)/shard_map/scatter/pallas_call | solution.py:379
  73.7 5.4 %collective-permute-start = (bf16[32,4096]{1,0:T(8,128)(2,1)S(1)}, bf16[32,4096]{1,0:T(8,128)(2,1)S(1)}, u32[]{:S(2)}, u32[]{:S(2)}) collective-permute-start(bf16[32,4096]{1,0:T(8,128)(2,1)S(1)} %scatter.3), channel_id=1, source_target_pairs={{0,64},{32,96},{64,0},{96,32},{1,65},{33,97},{65,1},{97,33},{2,66}... | collective-permute-start | bytes 786440 | tf_op jit(solution)/shard_map/ppermute | solution.py:427
  79.1 2.4 %scatter.5 = (bf16[32,4096]{1,0:T(8,128)(2,1)S(1)}, bf16[32,4096]{1,0:T(8,128)(2,1)S(1)}) custom-call(s32[1]{0:T(128)} %bitcast.2.refs_0_, f32[32,16384]{1,0:T(8,128)S(1)} %spread.1.refs_1_, bf16[32,64,128]{2,1,0:T(8,128)(2,1)S(1)} %all-to-all-done.2.back_ref.refs_2_, f32[8,4096]{1,0:T(8,128)S(1)} %get-tuple-element.27.refs_3_), custom_call_target="tpu_custom_call" | custom-call | flops 3460300800 | bytes 11010048 | tf_op jit(solution)/shard_map/scatter/pallas_call | solution.py:379
  81.5 1.1 collective-permute-start.1
  82.6 2.2 %collective-permute-start.2 = (bf16[32,4096]{1,0:T(8,128)(2,1)S(1)}, bf16[32,4096]{1,0:T(8,128)(2,1)S(1)}, u32[]{:S(2)}, u32[]{:S(2)}) collective-permute-start(bf16[32,4096]{1,0:T(8,128)(2,1)S(1)} %get-tuple-element.33), channel_id=1, source_target_pairs={{0,96},{32,0},{64,32},{96,64},{1,97},{33,1},{65,33},{97,65},{2,98}... | collective-permute-start | bytes 786440 | tf_op jit(solution)/shard_map/ppermute | solution.py:427
  84.8 1.4 %collective-permute-done.refs_4_ = bf16[32,4096]{1,0:T(8,128)(2,1)S(1)} collective-permute-done((bf16[32,4096]{1,0:T(8,128)(2,1)S(1)}, bf16[32,4096]{1,0:T(8,128)(2,1)S(1)}, u32[]{:S(2)}, u32[]{:S(2)}) %collective-permute-start) | collective-permute-done | bytes 262176 | tf_op jit(solution)/shard_map/ppermute | solution.py:427
  86.2 1.3 %scatter.4 = f32[32,4096]{1,0:T(8,128)S(1)} custom-call(s32[1]{0:T(128)} %bitcast.2.refs_0_, f32[32,16384]{1,0:T(8,128)S(1)} %spread.1.refs_1_, bf16[32,64,128]{2,1,0:T(8,128)(2,1)S(1)} %all-to-all-done.2.back_ref.refs_2_, f32[8,4096]{1,0:T(8,128)S(1)} %get-tuple-element.27.refs_3_, bf16[32,4096]{1,0:T(8,128)(2,1)S(1)} %collective-permute-done.refs_4_), custom_call_target="tpu_custom_call" | custom-call | flops 17301504000 | bytes 55050240 | tf_op jit(solution)/shard_map/scatter/pallas_call | solution.py:379
  87.5 1.5 %convert_reduce_fusion = f32[72,256]{1,0:T(8,128)S(1)} fusion(bf16[32,80,256]{2,1,0:T(8,128)(2,1)} %all-to-all-done.3), kind=kLoop, calls=%fused_computation | loop fusion | flops 1161216 | bytes 1253376 | tf_op jit(solution)/shard_map/reduce_sum | solution.py:470
  89.0 3.8 %collective-permute-start.8 = (f32[72,256]{1,0:T(8,128)S(1)}, f32[72,256]{1,0:T(8,128)S(1)}, u32[]{:S(2)}, u32[]{:S(2)}) collective-permute-start(f32[72,256]{1,0:T(8,128)S(1)} %convert_reduce_fusion), channel_id=1, source_target_pairs={{0,96},{32,0},{64,32},{96,64},{1,97},{33,1},{65,33},{97,65},{2,98}... | collective-permute-start | bytes 221192 | tf_op jit(solution)/shard_map/ppermute | solution.py:427
  92.8 1.9 %collective-permute-start.6 = (f32[72,256]{1,0:T(8,128)S(1)}, f32[72,256]{1,0:T(8,128)S(1)}, u32[]{:S(2)}, u32[]{:S(2)}) collective-permute-start(f32[72,256]{1,0:T(8,128)S(1)} %convert_reduce_fusion), channel_id=1, source_target_pairs={{0,64},{32,96},{64,0},{96,32},{1,65},{33,97},{65,1},{97,33},{2,66}... | collective-permute-start | bytes 221192 | tf_op jit(solution)/shard_map/ppermute | solution.py:427
  94.8 1.7 %collective-permute-start.5 = (bf16[32,4096]{1,0:T(8,128)(2,1)S(1)}, bf16[32,4096]{1,0:T(8,128)(2,1)S(1)}, u32[]{:S(2)}, u32[]{:S(2)}) collective-permute-start(bf16[32,4096]{1,0:T(8,128)(2,1)S(1)} %add_convert_fusion.refs_1_), channel_id=1, source_target_pairs={{0,64},{32,96},{64,0},{96,32},{1,65},{33,97},{65,1},{97,33},{2,66}... | collective-permute-start | bytes 786440 | tf_op jit(solution)/shard_map/ppermute | solution.py:427
  96.5 0.6 collective-permute-start.4
  97.1 1.8 %collective-permute-done.8 = f32[72,256]{1,0:T(8,128)S(1)} collective-permute-done((f32[72,256]{1,0:T(8,128)S(1)}, f32[72,256]{1,0:T(8,128)S(1)}, u32[]{:S(2)}, u32[]{:S(2)}) %collective-permute-start.8) | collective-permute-done | bytes 73760 | tf_op jit(solution)/shard_map/ppermute | solution.py:427
  99.0 4.2 %collective-permute-start.3 = (bf16[32,4096]{1,0:T(8,128)(2,1)S(1)}, bf16[32,4096]{1,0:T(8,128)(2,1)S(1)}, u32[]{:S(2)}, u32[]{:S(2)}) collective-permute-start(bf16[32,4096]{1,0:T(8,128)(2,1)S(1)} %add_convert_fusion.refs_1_), channel_id=1, source_target_pairs={{0,96},{32,0},{64,32},{96,64},{1,97},{33,1},{65,33},{97,65},{2,98}... | collective-permute-start | bytes 786440 | tf_op jit(solution)/shard_map/ppermute | solution.py:427
  103.1 1.1 collective-permute-done.7
  104.3 0.6 fusion.1
  104.9 0.6 fusion
  105.6 1.0 place_quarters.2.refs_3_
  106.6 3.2 %collective-permute-done.4.refs_2_ = bf16[32,4096]{1,0:T(8,128)(2,1)S(1)} collective-permute-done((bf16[32,4096]{1,0:T(8,128)(2,1)S(1)}, bf16[32,4096]{1,0:T(8,128)(2,1)S(1)}, u32[]{:S(2)}, u32[]{:S(2)}) %collective-permute-start.4) | collective-permute-done | bytes 262176 | tf_op jit(solution)/shard_map/ppermute | solution.py:427
  109.8 1.0 place_quarters.3
  (24 shorter events, 0.3 us)
Async XLA Ops:
  0.6 9.4 %copy-start.6 = (s32[1,32,16]{1,2,0:T(8,128)S(1)}, s32[1,32,16]{1,2,0:T(8,128)}, u32[]{:S(2)}) copy-start(s32[1,32,16]{1,2,0:T(8,128)} %param.12) | copy-start | bytes 6148
  0.6 9.5 %copy-start.3 = (s32[1,4096]{1,0:T(1,128)S(1)}, s32[1,4096]{1,0:T(1,128)}, u32[]{:S(2)}) copy-start(s32[1,4096]{1,0:T(1,128)} %slot_ref.3) | copy-start | bytes 49156
  0.7 9.4 %copy-start.5 = (s32[1,32]{1,0:T(1,128)S(1)}, s32[1,32]{1,0:T(1,128)}, u32[]{:S(2)}) copy-start(s32[1,32]{1,0:T(1,128)} %cnt_ref.3) | copy-start | bytes 388
  0.7 9.4 %copy-start.2 = (s32[1,4096]{1,0:T(1,128)S(1)}, s32[1,4096]{1,0:T(1,128)}, u32[]{:S(2)}) copy-start(s32[1,4096]{1,0:T(1,128)} %tgt_ref.1) | copy-start | bytes 49156
  0.7 9.4 %copy-start = (bf16[32,16384]{1,0:T(8,128)(2,1)S(1)}, bf16[32,16384]{1,0:T(8,128)(2,1)}, u32[]{:S(2)}) copy-start(bf16[32,16384]{1,0:T(8,128)(2,1)} %feat_ref.1) | copy-start | bytes 3145732
  2.6 24.7 %all-to-all-start = ((bf16[32,64,256]{2,1,0:T(8,128)(2,1)}), bf16[32,64,256]{2,1,0:T(8,128)(2,1)S(1)}, u32[]{:S(2)}, u32[]{:S(2)}) async-start(bf16[32,64,256]{2,1,0:T(8,128)(2,1)} %broadcast_in_dim.2), calls=%async_computation | async-start | bytes 2097152 | tf_op jit(solution)/shard_map/all_to_all | solution.py:431
  10.1 32.3 %copy-start.1 = (bf16[1,128,256]{2,1,0:T(8,128)(2,1)S(1)}, bf16[1,128,256]{2,1,0:T(8,128)(2,1)}, u32[]{:S(2)}) copy-start(bf16[1,128,256]{2,1,0:T(8,128)(2,1)} %grad_ref.1) | copy-start | bytes 196612
  10.1 32.3 %copy-start.4 = (f32[256]{0:T(256)S(1)}, f32[256]{0:T(256)}, u32[]{:S(2)}) copy-start(f32[256]{0:T(256)} %param.18) | copy-start | bytes 3076
  44.3 15.7 %all-to-all-start.2 = ((bf16[32,64,128]{2,1,0:T(8,128)(2,1)}), bf16[32,64,128]{2,1,0:T(8,128)(2,1)S(1)}, u32[]{:S(2)}, u32[]{:S(2)}) async-start(bf16[32,64,128]{2,1,0:T(8,128)(2,1)} %get-tuple-element.24), calls=%async_computation.2 | async-start | bytes 1048576 | tf_op jit(solution)/shard_map/all_to_all | solution.py:431
  59.9 27.6 %all-to-all-start.3 = ((bf16[32,80,256]{2,1,0:T(8,128)(2,1)}), bf16[32,80,256]{2,1,0:T(8,128)(2,1)}, u32[]{:S(2)}, u32[]{:S(2)}) async-start(bf16[32,80,256]{2,1,0:T(8,128)(2,1)} %weight_partials.1), calls=%async_computation.3 | async-start | bytes 2621440 | tf_op jit(solution)/shard_map/all_to_all | solution.py:431
  73.7 12.5 %collective-permute-start = (bf16[32,4096]{1,0:T(8,128)(2,1)S(1)}, bf16[32,4096]{1,0:T(8,128)(2,1)S(1)}, u32[]{:S(2)}, u32[]{:S(2)}) collective-permute-start(bf16[32,4096]{1,0:T(8,128)(2,1)S(1)} %scatter.3), channel_id=1, source_target_pairs={{0,64},{32,96},{64,0},{96,32},{1,65},{33,97},{65,1},{97,33},{2,66}... | collective-permute-start | bytes 786440 | tf_op jit(solution)/shard_map/ppermute | solution.py:427
  81.5 13.2 %collective-permute-start.1 = (bf16[32,4096]{1,0:T(8,128)(2,1)S(1)}, bf16[32,4096]{1,0:T(8,128)(2,1)S(1)}, u32[]{:S(2)}, u32[]{:S(2)}) collective-permute-start(bf16[32,4096]{1,0:T(8,128)(2,1)S(1)} %get-tuple-element.32), channel_id=1, source_target_pairs={{0,32},{32,64},{64,96},{96,0},{1,33},{33,65},{65,97},{97,1},{2,34}... | collective-permute-start | bytes 786440 | tf_op jit(solution)/shard_map/ppermute | solution.py:427
  82.6 12.1 %collective-permute-start.2 = (bf16[32,4096]{1,0:T(8,128)(2,1)S(1)}, bf16[32,4096]{1,0:T(8,128)(2,1)S(1)}, u32[]{:S(2)}, u32[]{:S(2)}) collective-permute-start(bf16[32,4096]{1,0:T(8,128)(2,1)S(1)} %get-tuple-element.33), channel_id=1, source_target_pairs={{0,96},{32,0},{64,32},{96,64},{1,97},{33,1},{65,33},{97,65},{2,98}... | collective-permute-start | bytes 786440 | tf_op jit(solution)/shard_map/ppermute | solution.py:427
  89.0 10.0 %collective-permute-start.8 = (f32[72,256]{1,0:T(8,128)S(1)}, f32[72,256]{1,0:T(8,128)S(1)}, u32[]{:S(2)}, u32[]{:S(2)}) collective-permute-start(f32[72,256]{1,0:T(8,128)S(1)} %convert_reduce_fusion), channel_id=1, source_target_pairs={{0,96},{32,0},{64,32},{96,64},{1,97},{33,1},{65,33},{97,65},{2,98}... | collective-permute-start | bytes 221192 | tf_op jit(solution)/shard_map/ppermute | solution.py:427
  92.8 11.5 %collective-permute-start.7 = (f32[72,256]{1,0:T(8,128)S(1)}, f32[72,256]{1,0:T(8,128)S(1)}, u32[]{:S(2)}, u32[]{:S(2)}) collective-permute-start(f32[72,256]{1,0:T(8,128)S(1)} %convert_reduce_fusion), channel_id=1, source_target_pairs={{0,32},{32,64},{64,96},{96,0},{1,33},{33,65},{65,97},{97,1},{2,34}... | collective-permute-start | bytes 221192 | tf_op jit(solution)/shard_map/ppermute | solution.py:427
  92.8 11.5 %collective-permute-start.6 = (f32[72,256]{1,0:T(8,128)S(1)}, f32[72,256]{1,0:T(8,128)S(1)}, u32[]{:S(2)}, u32[]{:S(2)}) collective-permute-start(f32[72,256]{1,0:T(8,128)S(1)} %convert_reduce_fusion), channel_id=1, source_target_pairs={{0,64},{32,96},{64,0},{96,32},{1,65},{33,97},{65,1},{97,33},{2,66}... | collective-permute-start | bytes 221192 | tf_op jit(solution)/shard_map/ppermute | solution.py:427
  94.8 10.8 %collective-permute-start.5 = (bf16[32,4096]{1,0:T(8,128)(2,1)S(1)}, bf16[32,4096]{1,0:T(8,128)(2,1)S(1)}, u32[]{:S(2)}, u32[]{:S(2)}) collective-permute-start(bf16[32,4096]{1,0:T(8,128)(2,1)S(1)} %add_convert_fusion.refs_1_), channel_id=1, source_target_pairs={{0,64},{32,96},{64,0},{96,32},{1,65},{33,97},{65,1},{97,33},{2,66}... | collective-permute-start | bytes 786440 | tf_op jit(solution)/shard_map/ppermute | solution.py:427
  96.5 13.3 %collective-permute-start.4 = (bf16[32,4096]{1,0:T(8,128)(2,1)S(1)}, bf16[32,4096]{1,0:T(8,128)(2,1)S(1)}, u32[]{:S(2)}, u32[]{:S(2)}) collective-permute-start(bf16[32,4096]{1,0:T(8,128)(2,1)S(1)} %add_convert_fusion.refs_1_), channel_id=1, source_target_pairs={{0,32},{32,64},{64,96},{96,0},{1,33},{33,65},{65,97},{97,1},{2,34}... | collective-permute-start | bytes 786440 | tf_op jit(solution)/shard_map/ppermute | solution.py:427
  99.0 10.8 %collective-permute-start.3 = (bf16[32,4096]{1,0:T(8,128)(2,1)S(1)}, bf16[32,4096]{1,0:T(8,128)(2,1)S(1)}, u32[]{:S(2)}, u32[]{:S(2)}) collective-permute-start(bf16[32,4096]{1,0:T(8,128)(2,1)S(1)} %add_convert_fusion.refs_1_), channel_id=1, source_target_pairs={{0,96},{32,0},{64,32},{96,64},{1,97},{33,1},{65,33},{97,65},{2,98}... | collective-permute-start | bytes 786440 | tf_op jit(solution)/shard_map/ppermute | solution.py:427

commit v4 on v3

--- a/solution.py
+++ b/solution.py
@@ -14,9 +14,9 @@
 COLS = 32
 FEAT = 32
 WIDE = 256
-CHUNK = 4
+CHUNK = 2
 PER = MAXB // CHUNK
-UNROLL = 16
+UNROLL = 32
 LOW = 512
 GROUP = 32
 LIST = TB * PER + UNROLL
@@ -47,7 +47,7 @@
         return pltpu.make_async_copy(tiles_ref.at[span], buf_ref.at[span], sem_ref.at[chunk])
 
     def block(b, total):
-        chunks = (cnt_ref[0, b] + (CHUNK - 1)) >> 2
+        chunks = (cnt_ref[0, b] + (CHUNK - 1)) >> 1
         for k in range(PER):
             list_ref[total + k] = b * PER + k
 
@@ -74,7 +74,7 @@
 
 def chunk_slots(bid_ref, cnt_ref, list_ref, item, total):
     chunk = list_ref[item]
-    block = chunk >> 2
+    block = chunk >> 3
     first = (chunk & (PER - 1)) * CHUNK
     count = jnp.where(item < total, cnt_ref[0, block], 0)
     slots = [(bid_ref[0, block, first + j], first + j < count) for j in range(CHUNK)]
@@ -162,7 +162,7 @@
             agg_ref[:, span] += prod
         return carry
 
-    lax.fori_loop(0, (total + UNROLL - 1) >> 4, aggregate, 0)
+    lax.fori_loop(0, (total + UNROLL - 1) >> 5, aggregate, 0)
 
     aggregate_rows = agg_ref[...].astype(BF16)
     half = 8
@@ -329,7 +329,7 @@
                 grad_ref[:, span] += jnp.where(live, piece, 0.0)
         return carry
 
-    lax.fori_loop(0, (total + UNROLL - 1) >> 4, spread, 0)
+    lax.fori_loop(0, (total + UNROLL - 1) >> 5, spread, 0)
 
 
 def spread_part(block_ids, counts, back, slots, tiles):

time: 112 us -> 115 us (1.027); the launches traced: 111 us -> 116 us
  Pallas kernels: 31.2 us -> 35.3 us
  waiting for transfers between devices: 22 us -> 19.8 us
  blocking collectives: 15.1 us -> 17 us
    all_to_all x3, waiting for transfers between devices: 14.4 us -> 12.3 us  [exchange(): return lax.all_to_all(value, 'feat', 0, 0, tiled=True)]
    pallas_call x1, Pallas kernels: 13.1 us -> 15.2 us  [forward(): pl.pallas_call(forward_kernel, out_shape=(BLOCKS, jax.ShapeDtypeStruct((8...]
    pallas_call x1, Pallas kernels: 7.81 us -> 9.84 us  [spread_part(): pl.pallas_call(spread_kernel, out_shape=jax.ShapeDtypeStruct((COLS, NODES...]
    all_to_all x1, blocking collectives: 15.1 us -> 17 us  [exchange(): return lax.all_to_all(value, 'feat', 0, 0, tiled=True)]
  transfers between devices with their start and end apart: 12 -> 12, of which waited for: 7 -> 7; matrix products, arithmetic and copies ran while one was open for 3% -> 2% of each run, Pallas kernels for 26% -> 28%
where the time goes in v4:
time: 115 us; the launch traced here: 116 us
  starting transfers between devices  37.6 us (33%)
  Pallas kernels  35.3 us (31%)
  waiting for transfers between devices  19.8 us (17%)
  blocking collectives  17 us (15%)
  other arithmetic  2.95 us (3%)
  local copies, waits for them, and re-layouts  1.83 us (2%)
    ppermute x9, starting transfers between devices, shift(): return lax.ppermute(value, 'dp', [(k, (k + by) % 4) for k in range(4)])  21.7 us
    all_to_all x1, blocking collectives, exchange(): return lax.all_to_all(value, 'feat', 0, 0, tiled=True)  17 us
    all_to_all x3, starting transfers between devices, exchange(): return lax.all_to_all(value, 'feat', 0, 0, tiled=True)  16 us
    pallas_call x1, Pallas kernels, forward(): pl.pallas_call(forward_kernel, out_shape=(BLOCKS, jax.ShapeDtypeStruct((8...  15.2 us
    all_to_all x3, waiting for transfers between devices, exchange(): return lax.all_to_all(value, 'feat', 0, 0, tiled=True)  12.3 us
    pallas_call x1, Pallas kernels, spread_part(): pl.pallas_call(spread_kernel, out_shape=jax.ShapeDtypeStruct((COLS, NODES...  9.84 us
    ppermute x9, waiting for transfers between devices, shift(): return lax.ppermute(value, 'dp', [(k, (k + by) % 4) for k in range(4)])  7.59 us
    pallas_call x3, Pallas kernels, scatter_part(): pl.pallas_call(lambda *refs: scatter_kernel(*refs, steps=steps, plus=len(...  4.95 us
  transfers between devices with their start and end apart: 12, of which 7 were waited for; matrix products, arithmetic and copies ran while one was open for 2% of the time, Pallas kernels for 28%

profile of v4, /device:TPU:0, one launch (start us, length us, event | category | flops | bytes accessed | tf_op | source)
XLA Modules:
  0.0 115.5 jit_solution(5351769540500310654)
XLA Ops:
  0.7 0.8 pad_maximum_fusion
  1.5 1.1 broadcast_in_dim.2
  2.6 7.4 %all-to-all-start = ((bf16[32,64,256]{2,1,0:T(8,128)(2,1)}), bf16[32,64,256]{2,1,0:T(8,128)(2,1)S(1)}, u32[]{:S(2)}, u32[]{:S(2)}) async-start(bf16[32,64,256]{2,1,0:T(8,128)(2,1)} %broadcast_in_dim.2), calls=%async_computation | async-start | bytes 2097152 | tf_op jit(solution)/shard_map/all_to_all | solution.py:431
  10.1 15.2 %gather_and_aggregate.1 = (bf16[32,64,128]{2,1,0:T(8,128)(2,1)S(1)}, f32[8,4096]{1,0:T(8,128)S(1)}) custom-call(s32[1,32,16]{2,1,0:T(8,128)S(1)} %copy.16.bid_ref, s32[1,32]{1,0:T(1,128)S(1)} %copy-done.5, bf16[32,16384]{1,0:T(8,128)(2,1)S(1)} %copy-done, s32[1,4096]{1,0:T(1,128)S(1)} %copy-done.2, s32[1,4096]{1,0:T(1,128)S(1)} %copy-done.3, ...), custom_call_target="tpu_custom_call" | custom-call | flops 17301504000 | bytes 55050240 | tf_op jit(solution)/shard_map/gather_and_aggregate/pallas_call | solution.py:208
  25.4 2.0 %all-to-all-done.w_ref = bf16[32,64,256]{2,1,0:T(8,128)(2,1)S(1)} async-done(((bf16[32,64,256]{2,1,0:T(8,128)(2,1)}), bf16[32,64,256]{2,1,0:T(8,128)(2,1)S(1)}, u32[]{:S(2)}, u32[]{:S(2)}) %all-to-all-start) | async-done | bytes 1048608 | tf_op jit(solution)/shard_map/all_to_all | solution.py:431
  27.3 17.0 %all_to_all.20.x_ref = bf16[32,64,128]{2,1,0:T(8,128)(2,1)S(1)} all-to-all(bf16[32,64,128]{2,1,0:T(8,128)(2,1)S(1)} %get-tuple-element.21), channel_id=1, replica_groups=mesh['dp'=4,'feat'=32] {'feat'}, dimensions={0} | all-to-all | bytes 1048576 | tf_op jit(solution)/shard_map/all_to_all | solution.py:431
  44.3 1.8 %hidden_and_slope.1 = (bf16[1,128,256]{2,1,0:T(8,128)(2,1)}, bf16[32,64,128]{2,1,0:T(8,128)(2,1)}, bf16[128,256]{1,0:T(8,128)(2,1)S(1)}) custom-call(bf16[32,64,128]{2,1,0:T(8,128)(2,1)S(1)} %all_to_all.20.x_ref, bf16[32,64,256]{2,1,0:T(8,128)(2,1)S(1)} %all-to-all-done.w_ref, f32[1,256]{1,0:T(1,128)S(1)} %bitcast.4, bf16[1,128,256]{2,1,0:T(8,128)(2,1)S(1)} %copy-done.1), custom_call_target="tpu_custom_call" | custom-call | flops 2306867200 | bytes 7340032 | tf_op jit(solution)/shard_map/hidden_and_slope/pallas_call | solution.py:276
  46.1 3.9 %all-to-all-start.2 = ((bf16[32,64,128]{2,1,0:T(8,128)(2,1)}), bf16[32,64,128]{2,1,0:T(8,128)(2,1)S(1)}, u32[]{:S(2)}, u32[]{:S(2)}) async-start(bf16[32,64,128]{2,1,0:T(8,128)(2,1)} %get-tuple-element.24), calls=%async_computation.2 | async-start | bytes 1048576 | tf_op jit(solution)/shard_map/all_to_all | solution.py:431
  50.0 1.5 %weight_partials.1 = bf16[32,80,256]{2,1,0:T(8,128)(2,1)} custom-call(bf16[32,64,128]{2,1,0:T(8,128)(2,1)S(1)} %all_to_all.20.x_ref, bf16[128,256]{1,0:T(8,128)(2,1)S(1)} %get-tuple-element.25.slope_ref), custom_call_target="tpu_custom_call" | custom-call | flops 2306867200 | bytes 7340032 | tf_op jit(solution)/shard_map/weight_partials/pallas_call | solution.py:264
  51.5 10.3 %all-to-all-done.2.back_ref.refs_2_ = bf16[32,64,128]{2,1,0:T(8,128)(2,1)S(1)} async-done(((bf16[32,64,128]{2,1,0:T(8,128)(2,1)}), bf16[32,64,128]{2,1,0:T(8,128)(2,1)S(1)}, u32[]{:S(2)}, u32[]{:S(2)}) %all-to-all-start.2) | async-done | bytes 524320 | tf_op jit(solution)/shard_map/all_to_all | solution.py:431
  61.8 4.7 %all-to-all-start.3 = ((bf16[32,80,256]{2,1,0:T(8,128)(2,1)}), bf16[32,80,256]{2,1,0:T(8,128)(2,1)}, u32[]{:S(2)}, u32[]{:S(2)}) async-start(bf16[32,80,256]{2,1,0:T(8,128)(2,1)} %weight_partials.1), calls=%async_computation.3 | async-start | bytes 2621440 | tf_op jit(solution)/shard_map/all_to_all | solution.py:431
  66.5 9.8 %spread.1.refs_1_ = f32[32,16384]{1,0:T(8,128)S(1)} custom-call(s32[1,32,16]{2,1,0:T(8,128)S(1)} %copy.16.bid_ref, s32[1,32]{1,0:T(1,128)S(1)} %copy-done.5, bf16[32,64,128]{2,1,0:T(8,128)(2,1)S(1)} %all-to-all-done.2.back_ref.refs_2_, s32[1,4096]{1,0:T(1,128)S(1)} %copy-done.3, bf16[512,128,128]{2,1,0:T(8,128)(2,1)} %bitcast.7), custom_call_target="tpu_custom_call" | custom-call | flops 8074035200 | bytes 25690112 | tf_op jit(solution)/shard_map/spread/pallas_call | solution.py:336
  76.3 1.3 %scatter.3 = bf16[32,4096]{1,0:T(8,128)(2,1)S(1)} custom-call(s32[1]{0:T(128)} %bitcast.2.refs_0_, f32[32,16384]{1,0:T(8,128)S(1)} %spread.1.refs_1_, bf16[32,64,128]{2,1,0:T(8,128)(2,1)S(1)} %all-to-all-done.2.back_ref.refs_2_, f32[8,4096]{1,0:T(8,128)S(1)} %get-tuple-element.27.refs_3_), custom_call_target="tpu_custom_call" | custom-call | flops 2306867200 | bytes 7340032 | tf_op jit(solution)/shard_map/scatter/pallas_call | solution.py:379
  77.6 6.0 %collective-permute-start = (bf16[32,4096]{1,0:T(8,128)(2,1)S(1)}, bf16[32,4096]{1,0:T(8,128)(2,1)S(1)}, u32[]{:S(2)}, u32[]{:S(2)}) collective-permute-start(bf16[32,4096]{1,0:T(8,128)(2,1)S(1)} %scatter.3), channel_id=1, source_target_pairs={{0,64},{32,96},{64,0},{96,32},{1,65},{33,97},{65,1},{97,33},{2,66}... | collective-permute-start | bytes 786440 | tf_op jit(solution)/shard_map/ppermute | solution.py:427
  83.7 2.4 %scatter.5 = (bf16[32,4096]{1,0:T(8,128)(2,1)S(1)}, bf16[32,4096]{1,0:T(8,128)(2,1)S(1)}) custom-call(s32[1]{0:T(128)} %bitcast.2.refs_0_, f32[32,16384]{1,0:T(8,128)S(1)} %spread.1.refs_1_, bf16[32,64,128]{2,1,0:T(8,128)(2,1)S(1)} %all-to-all-done.2.back_ref.refs_2_, f32[8,4096]{1,0:T(8,128)S(1)} %get-tuple-element.27.refs_3_), custom_call_target="tpu_custom_call" | custom-call | flops 3460300800 | bytes 11010048 | tf_op jit(solution)/shard_map/scatter/pallas_call | solution.py:379
  86.1 1.2 collective-permute-start.1
  87.2 2.3 %collective-permute-start.2 = (bf16[32,4096]{1,0:T(8,128)(2,1)S(1)}, bf16[32,4096]{1,0:T(8,128)(2,1)S(1)}, u32[]{:S(2)}, u32[]{:S(2)}) collective-permute-start(bf16[32,4096]{1,0:T(8,128)(2,1)S(1)} %get-tuple-element.33), channel_id=1, source_target_pairs={{0,96},{32,0},{64,32},{96,64},{1,97},{33,1},{65,33},{97,65},{2,98}... | collective-permute-start | bytes 786440 | tf_op jit(solution)/shard_map/ppermute | solution.py:427
  89.5 1.2 %collective-permute-done.refs_4_ = bf16[32,4096]{1,0:T(8,128)(2,1)S(1)} collective-permute-done((bf16[32,4096]{1,0:T(8,128)(2,1)S(1)}, bf16[32,4096]{1,0:T(8,128)(2,1)S(1)}, u32[]{:S(2)}, u32[]{:S(2)}) %collective-permute-start) | collective-permute-done | bytes 262176 | tf_op jit(solution)/shard_map/ppermute | solution.py:427
  90.8 1.3 %scatter.4 = f32[32,4096]{1,0:T(8,128)S(1)} custom-call(s32[1]{0:T(128)} %bitcast.2.refs_0_, f32[32,16384]{1,0:T(8,128)S(1)} %spread.1.refs_1_, bf16[32,64,128]{2,1,0:T(8,128)(2,1)S(1)} %all-to-all-done.2.back_ref.refs_2_, f32[8,4096]{1,0:T(8,128)S(1)} %get-tuple-element.27.refs_3_, bf16[32,4096]{1,0:T(8,128)(2,1)S(1)} %collective-permute-done.refs_4_), custom_call_target="tpu_custom_call" | custom-call | flops 17301504000 | bytes 55050240 | tf_op jit(solution)/shard_map/scatter/pallas_call | solution.py:379
  92.1 1.5 %convert_reduce_fusion = f32[72,256]{1,0:T(8,128)S(1)} fusion(bf16[32,80,256]{2,1,0:T(8,128)(2,1)} %all-to-all-done.3), kind=kLoop, calls=%fused_computation | loop fusion | flops 1161216 | bytes 1253376 | tf_op jit(solution)/shard_map/reduce_sum | solution.py:470
  93.5 3.7 %collective-permute-start.8 = (f32[72,256]{1,0:T(8,128)S(1)}, f32[72,256]{1,0:T(8,128)S(1)}, u32[]{:S(2)}, u32[]{:S(2)}) collective-permute-start(f32[72,256]{1,0:T(8,128)S(1)} %convert_reduce_fusion), channel_id=1, source_target_pairs={{0,96},{32,0},{64,32},{96,64},{1,97},{33,1},{65,33},{97,65},{2,98}... | collective-permute-start | bytes 221192 | tf_op jit(solution)/shard_map/ppermute | solution.py:427
  97.2 2.0 %collective-permute-start.6 = (f32[72,256]{1,0:T(8,128)S(1)}, f32[72,256]{1,0:T(8,128)S(1)}, u32[]{:S(2)}, u32[]{:S(2)}) collective-permute-start(f32[72,256]{1,0:T(8,128)S(1)} %convert_reduce_fusion), channel_id=1, source_target_pairs={{0,64},{32,96},{64,0},{96,32},{1,65},{33,97},{65,1},{97,33},{2,66}... | collective-permute-start | bytes 221192 | tf_op jit(solution)/shard_map/ppermute | solution.py:427
  99.3 1.6 %collective-permute-start.5 = (bf16[32,4096]{1,0:T(8,128)(2,1)S(1)}, bf16[32,4096]{1,0:T(8,128)(2,1)S(1)}, u32[]{:S(2)}, u32[]{:S(2)}) collective-permute-start(bf16[32,4096]{1,0:T(8,128)(2,1)S(1)} %add_convert_fusion.refs_1_), channel_id=1, source_target_pairs={{0,64},{32,96},{64,0},{96,32},{1,65},{33,97},{65,1},{97,33},{2,66}... | collective-permute-start | bytes 786440 | tf_op jit(solution)/shard_map/ppermute | solution.py:427
  100.9 0.6 collective-permute-start.4
  101.6 1.8 %collective-permute-done.8 = f32[72,256]{1,0:T(8,128)S(1)} collective-permute-done((f32[72,256]{1,0:T(8,128)S(1)}, f32[72,256]{1,0:T(8,128)S(1)}, u32[]{:S(2)}, u32[]{:S(2)}) %collective-permute-start.8) | collective-permute-done | bytes 73760 | tf_op jit(solution)/shard_map/ppermute | solution.py:427
  103.4 4.2 %collective-permute-start.3 = (bf16[32,4096]{1,0:T(8,128)(2,1)S(1)}, bf16[32,4096]{1,0:T(8,128)(2,1)S(1)}, u32[]{:S(2)}, u32[]{:S(2)}) collective-permute-start(bf16[32,4096]{1,0:T(8,128)(2,1)S(1)} %add_convert_fusion.refs_1_), channel_id=1, source_target_pairs={{0,96},{32,0},{64,32},{96,64},{1,97},{33,1},{65,33},{97,65},{2,98}... | collective-permute-start | bytes 786440 | tf_op jit(solution)/shard_map/ppermute | solution.py:427
  107.6 1.1 collective-permute-done.7
  108.7 0.6 fusion.1
  109.4 0.6 fusion
  110.2 1.0 place_quarters.2.refs_3_
  111.2 3.2 %collective-permute-done.4.refs_2_ = bf16[32,4096]{1,0:T(8,128)(2,1)S(1)} collective-permute-done((bf16[32,4096]{1,0:T(8,128)(2,1)S(1)}, bf16[32,4096]{1,0:T(8,128)(2,1)S(1)}, u32[]{:S(2)}, u32[]{:S(2)}) %collective-permute-start.4) | collective-permute-done | bytes 262176 | tf_op jit(solution)/shard_map/ppermute | solution.py:427
  114.4 1.0 place_quarters.3
  (24 shorter events, 0.4 us)
Async XLA Ops:
  0.6 9.4 %copy-start.6 = (s32[1,32,16]{1,2,0:T(8,128)S(1)}, s32[1,32,16]{1,2,0:T(8,128)}, u32[]{:S(2)}) copy-start(s32[1,32,16]{1,2,0:T(8,128)} %param.12) | copy-start | bytes 6148
  0.6 9.5 %copy-start.3 = (s32[1,4096]{1,0:T(1,128)S(1)}, s32[1,4096]{1,0:T(1,128)}, u32[]{:S(2)}) copy-start(s32[1,4096]{1,0:T(1,128)} %slot_ref.3) | copy-start | bytes 49156
  0.7 9.4 %copy-start.5 = (s32[1,32]{1,0:T(1,128)S(1)}, s32[1,32]{1,0:T(1,128)}, u32[]{:S(2)}) copy-start(s32[1,32]{1,0:T(1,128)} %cnt_ref.3) | copy-start | bytes 388
  0.7 9.4 %copy-start.2 = (s32[1,4096]{1,0:T(1,128)S(1)}, s32[1,4096]{1,0:T(1,128)}, u32[]{:S(2)}) copy-start(s32[1,4096]{1,0:T(1,128)} %tgt_ref.1) | copy-start | bytes 49156
  0.7 9.4 %copy-start = (bf16[32,16384]{1,0:T(8,128)(2,1)S(1)}, bf16[32,16384]{1,0:T(8,128)(2,1)}, u32[]{:S(2)}) copy-start(bf16[32,16384]{1,0:T(8,128)(2,1)} %feat_ref.1) | copy-start | bytes 3145732
  2.6 24.7 %all-to-all-start = ((bf16[32,64,256]{2,1,0:T(8,128)(2,1)}), bf16[32,64,256]{2,1,0:T(8,128)(2,1)S(1)}, u32[]{:S(2)}, u32[]{:S(2)}) async-start(bf16[32,64,256]{2,1,0:T(8,128)(2,1)} %broadcast_in_dim.2), calls=%async_computation | async-start | bytes 2097152 | tf_op jit(solution)/shard_map/all_to_all | solution.py:431
  10.1 34.2 %copy-start.1 = (bf16[1,128,256]{2,1,0:T(8,128)(2,1)S(1)}, bf16[1,128,256]{2,1,0:T(8,128)(2,1)}, u32[]{:S(2)}) copy-start(bf16[1,128,256]{2,1,0:T(8,128)(2,1)} %grad_ref.1) | copy-start | bytes 196612
  10.1 34.2 %copy-start.4 = (f32[256]{0:T(256)S(1)}, f32[256]{0:T(256)}, u32[]{:S(2)}) copy-start(f32[256]{0:T(256)} %param.18) | copy-start | bytes 3076
  46.1 15.7 %all-to-all-start.2 = ((bf16[32,64,128]{2,1,0:T(8,128)(2,1)}), bf16[32,64,128]{2,1,0:T(8,128)(2,1)S(1)}, u32[]{:S(2)}, u32[]{:S(2)}) async-start(bf16[32,64,128]{2,1,0:T(8,128)(2,1)} %get-tuple-element.24), calls=%async_computation.2 | async-start | bytes 1048576 | tf_op jit(solution)/shard_map/all_to_all | solution.py:431
  61.8 30.3 %all-to-all-start.3 = ((bf16[32,80,256]{2,1,0:T(8,128)(2,1)}), bf16[32,80,256]{2,1,0:T(8,128)(2,1)}, u32[]{:S(2)}, u32[]{:S(2)}) async-start(bf16[32,80,256]{2,1,0:T(8,128)(2,1)} %weight_partials.1), calls=%async_computation.3 | async-start | bytes 2621440 | tf_op jit(solution)/shard_map/all_to_all | solution.py:431
  77.6 13.2 %collective-permute-start = (bf16[32,4096]{1,0:T(8,128)(2,1)S(1)}, bf16[32,4096]{1,0:T(8,128)(2,1)S(1)}, u32[]{:S(2)}, u32[]{:S(2)}) collective-permute-start(bf16[32,4096]{1,0:T(8,128)(2,1)S(1)} %scatter.3), channel_id=1, source_target_pairs={{0,64},{32,96},{64,0},{96,32},{1,65},{33,97},{65,1},{97,33},{2,66}... | collective-permute-start | bytes 786440 | tf_op jit(solution)/shard_map/ppermute | solution.py:427
  86.1 13.2 %collective-permute-start.1 = (bf16[32,4096]{1,0:T(8,128)(2,1)S(1)}, bf16[32,4096]{1,0:T(8,128)(2,1)S(1)}, u32[]{:S(2)}, u32[]{:S(2)}) collective-permute-start(bf16[32,4096]{1,0:T(8,128)(2,1)S(1)} %get-tuple-element.32), channel_id=1, source_target_pairs={{0,32},{32,64},{64,96},{96,0},{1,33},{33,65},{65,97},{97,1},{2,34}... | collective-permute-start | bytes 786440 | tf_op jit(solution)/shard_map/ppermute | solution.py:427
  87.2 12.0 %collective-permute-start.2 = (bf16[32,4096]{1,0:T(8,128)(2,1)S(1)}, bf16[32,4096]{1,0:T(8,128)(2,1)S(1)}, u32[]{:S(2)}, u32[]{:S(2)}) collective-permute-start(bf16[32,4096]{1,0:T(8,128)(2,1)S(1)} %get-tuple-element.33), channel_id=1, source_target_pairs={{0,96},{32,0},{64,32},{96,64},{1,97},{33,1},{65,33},{97,65},{2,98}... | collective-permute-start | bytes 786440 | tf_op jit(solution)/shard_map/ppermute | solution.py:427
  93.5 9.9 %collective-permute-start.8 = (f32[72,256]{1,0:T(8,128)S(1)}, f32[72,256]{1,0:T(8,128)S(1)}, u32[]{:S(2)}, u32[]{:S(2)}) collective-permute-start(f32[72,256]{1,0:T(8,128)S(1)} %convert_reduce_fusion), channel_id=1, source_target_pairs={{0,96},{32,0},{64,32},{96,64},{1,97},{33,1},{65,33},{97,65},{2,98}... | collective-permute-start | bytes 221192 | tf_op jit(solution)/shard_map/ppermute | solution.py:427
  97.2 11.5 %collective-permute-start.7 = (f32[72,256]{1,0:T(8,128)S(1)}, f32[72,256]{1,0:T(8,128)S(1)}, u32[]{:S(2)}, u32[]{:S(2)}) collective-permute-start(f32[72,256]{1,0:T(8,128)S(1)} %convert_reduce_fusion), channel_id=1, source_target_pairs={{0,32},{32,64},{64,96},{96,0},{1,33},{33,65},{65,97},{97,1},{2,34}... | collective-permute-start | bytes 221192 | tf_op jit(solution)/shard_map/ppermute | solution.py:427
  97.2 11.5 %collective-permute-start.6 = (f32[72,256]{1,0:T(8,128)S(1)}, f32[72,256]{1,0:T(8,128)S(1)}, u32[]{:S(2)}, u32[]{:S(2)}) collective-permute-start(f32[72,256]{1,0:T(8,128)S(1)} %convert_reduce_fusion), channel_id=1, source_target_pairs={{0,64},{32,96},{64,0},{96,32},{1,65},{33,97},{65,1},{97,33},{2,66}... | collective-permute-start | bytes 221192 | tf_op jit(solution)/shard_map/ppermute | solution.py:427
  99.3 10.8 %collective-permute-start.5 = (bf16[32,4096]{1,0:T(8,128)(2,1)S(1)}, bf16[32,4096]{1,0:T(8,128)(2,1)S(1)}, u32[]{:S(2)}, u32[]{:S(2)}) collective-permute-start(bf16[32,4096]{1,0:T(8,128)(2,1)S(1)} %add_convert_fusion.refs_1_), channel_id=1, source_target_pairs={{0,64},{32,96},{64,0},{96,32},{1,65},{33,97},{65,1},{97,33},{2,66}... | collective-permute-start | bytes 786440 | tf_op jit(solution)/shard_map/ppermute | solution.py:427
  100.9 13.4 %collective-permute-start.4 = (bf16[32,4096]{1,0:T(8,128)(2,1)S(1)}, bf16[32,4096]{1,0:T(8,128)(2,1)S(1)}, u32[]{:S(2)}, u32[]{:S(2)}) collective-permute-start(bf16[32,4096]{1,0:T(8,128)(2,1)S(1)} %add_convert_fusion.refs_1_), channel_id=1, source_target_pairs={{0,32},{32,64},{64,96},{96,0},{1,33},{33,65},{65,97},{97,1},{2,34}... | collective-permute-start | bytes 786440 | tf_op jit(solution)/shard_map/ppermute | solution.py:427
  103.4 10.9 %collective-permute-start.3 = (bf16[32,4096]{1,0:T(8,128)(2,1)S(1)}, bf16[32,4096]{1,0:T(8,128)(2,1)S(1)}, u32[]{:S(2)}, u32[]{:S(2)}) collective-permute-start(bf16[32,4096]{1,0:T(8,128)(2,1)S(1)} %add_convert_fusion.refs_1_), channel_id=1, source_target_pairs={{0,96},{32,0},{64,32},{96,64},{1,97},{33,1},{65,33},{97,65},{2,98}... | collective-permute-start | bytes 786440 | tf_op jit(solution)/shard_map/ppermute | solution.py:427
